TPU v7x, 32 devices: a whole 2x2x4 slice. The times are simulated.
32 devices in a mesh: hid: 8 (over z, x), tok: 4 (over y, core).
Axes of the slice: x: 2, y: 2, z: 4, core: 2. Of those that a mesh axis runs over, the one named last changes fastest.
Arguments:
- tokens: bfloat16 [1024, 12288], P('tok', 'hid'), may hold values from -6 to 6
- cotangent: bfloat16 [1024, 12288], P('tok', 'hid'), may hold values from -0.75 to 0.75
- up_tiles: bfloat16 [4, 1024, 24576], P(None, None, 'hid'), may hold values from -0.09375 to 0.09375
- down_tiles: bfloat16 [4, 24576, 1024], P(None, 'hid'), may hold values from -0.0625 to 0.0625
- block_index: int32 [4, 96, 2], P(None, 'hid'), may hold values from 0 to 2, as said below
- up_left: bfloat16 [12288, 256], P('hid'), may hold values from -0.0546875 to 0.0546875
- up_right: bfloat16 [256, 24576], P(None, 'hid'), may hold values from -0.375 to 0.375
- down_left: bfloat16 [24576, 256], P('hid'), may hold values from -0.0390625 to 0.0390625
- down_right: bfloat16 [256, 12288], P(None, 'hid'), may hold values from -0.375 to 0.375
Outputs:
- layer_out: bfloat16 [1024, 12288], P('tok', 'hid')
- grad_tokens: bfloat16 [1024, 12288], P('tok', 'hid')
- grad_up_tiles: bfloat16 [4, 1024, 24576], P(None, 'tok', 'hid')
- grad_down_tiles: bfloat16 [4, 24576, 1024], P(None, ('hid', 'tok'))
- grad_up_left: bfloat16 [12288, 256], P(('hid', 'tok'))
- grad_up_right: bfloat16 [256, 24576], P('tok', 'hid')
- grad_down_left: bfloat16 [24576, 256], P(('hid', 'tok'))
- grad_down_right: bfloat16 [256, 12288], P('tok', 'hid')
Inputs may be any that keep to these rules, and one draw needn't show every extreme that they name: `block_index`: each row names two different sub-blocks.
All inputs are finite; a program needn't handle non-finite values.
Results may differ from a plain program's by a relative error of at most 0.03.
Values may be sent and summed in bfloat16 or wider, within the bound.
A program may use at most 320 MiB of HBM per device.

v0:
```python
import jax
import jax.numpy as jnp
from jax import lax
from jax.sharding import PartitionSpec as P

GELU_SCALE = 0.7978845608028654
GELU_CUBIC = 0.044715


def partner(block, axis, distance):
    count = lax.axis_size(axis)
    route = []
    for low in range(count):
        high = low | 1 << distance
        if high != low and high < count:
            route += [(low, high), (high, low)]
    return lax.ppermute(block, axis, route)


def gelu_parts(pre_act):
    inner = GELU_SCALE * (pre_act + GELU_CUBIC * pre_act * pre_act * pre_act)
    tanh_value = jnp.tanh(inner)
    value = 0.5 * pre_act * (1.0 + tanh_value)
    slope = 0.5 * (1.0 + tanh_value) + 0.5 * pre_act * (
        1.0 - tanh_value * tanh_value
    ) * GELU_SCALE * (1.0 + 3.0 * GELU_CUBIC * pre_act * pre_act)
    return (value, slope)


def on_device(
    tokens, cotangent, up_tiles, down_tiles, block_index, up_left, up_right, down_left, down_right
):
    hid_count = lax.axis_size("hid")
    level_count = hid_count.bit_length()
    token_rows, feat_width = tokens.shape
    sub_width = feat_width // 3
    block_count = block_index.shape[1]
    hidden_width = up_tiles.shape[2]
    block_width = hidden_width // block_count
    select_float_values = (block_index[..., None] == jnp.arange(3, dtype=jnp.int32)).astype(
        jnp.float32
    )
    select_half_values = select_float_values.astype(jnp.bfloat16)
    up_blocks = [
        up_tiles[partition_key].reshape(2, sub_width, block_count, block_width)
        for partition_key in range(level_count)
    ]
    down_blocks = [
        down_tiles[partition_key].reshape(block_count, block_width, 2, sub_width)
        for partition_key in range(level_count)
    ]

    def choose(field, partition_key):
        reshaped_tiles = field.reshape(token_rows, 3, sub_width)
        return jnp.einsum(
            "rfg,hyf->rhyg",
            reshaped_tiles,
            select_half_values[partition_key],
            preferred_element_type=jnp.float32,
        ).astype(jnp.bfloat16)

    def place(partner_pairs, partition_key):
        placed_blocks = jnp.einsum(
            "kdow,dog->kgw",
            partner_pairs,
            select_float_values[partition_key],
            precision=lax.Precision.HIGHEST,
        )
        return placed_blocks.reshape(token_rows, feat_width).astype(jnp.bfloat16)

    feature_copies = [tokens] + [
        partner(tokens, "hid", partition_key) for partition_key in range(level_count - 1)
    ]
    low_up = lax.psum(
        jnp.dot(tokens, up_left, preferred_element_type=jnp.float32).astype(jnp.bfloat16), "hid"
    )
    chosen_inputs = [
        choose(feature_copies[partition_key], partition_key) for partition_key in range(level_count)
    ]
    pre_act = jnp.dot(low_up, up_right, preferred_element_type=jnp.float32).reshape(
        token_rows, block_count, block_width
    )
    for partition_key in range(level_count):
        pre_act = pre_act + jnp.einsum(
            "tbjs,jsbh->tbh",
            chosen_inputs[partition_key],
            up_blocks[partition_key],
            preferred_element_type=jnp.float32,
        )
    hidden_value, slope = gelu_parts(pre_act)
    hidden_act = hidden_value.astype(jnp.bfloat16)
    hidden_flat = hidden_act.reshape(token_rows, hidden_width)
    low_down = lax.psum(
        jnp.dot(hidden_flat, down_left, preferred_element_type=jnp.float32).astype(jnp.bfloat16),
        "hid",
    )
    out_parts = [
        place(
            jnp.einsum(
                "tbh,bhjs->tbjs",
                hidden_act,
                down_blocks[partition_key],
                preferred_element_type=jnp.float32,
            ),
            partition_key,
        )
        for partition_key in range(level_count)
    ]
    output_acc = out_parts[0].astype(jnp.float32)
    for partition_key in range(1, level_count):
        output_acc = output_acc + partner(
            out_parts[partition_key], "hid", partition_key - 1
        ).astype(jnp.float32)
    layer_out = (
        output_acc + jnp.dot(low_down, down_right, preferred_element_type=jnp.float32)
    ).astype(jnp.bfloat16)
    back_down = lax.psum(
        jnp.dot(cotangent, down_right.T, preferred_element_type=jnp.float32).astype(jnp.bfloat16),
        "hid",
    )
    grad_copies = [cotangent] + [
        partner(cotangent, "hid", partition_key) for partition_key in range(level_count - 1)
    ]
    chosen_grads = [
        choose(grad_copies[partition_key], partition_key) for partition_key in range(level_count)
    ]
    grad_hidden = jnp.dot(back_down, down_left.T, preferred_element_type=jnp.float32).reshape(
        token_rows, block_count, block_width
    )
    for partition_key in range(level_count):
        grad_hidden = grad_hidden + jnp.einsum(
            "tbjs,bhjs->tbh",
            chosen_grads[partition_key],
            down_blocks[partition_key],
            preferred_element_type=jnp.float32,
        )
    down_terms = jnp.stack(
        [
            jnp.einsum(
                "tbh,tbjs->bhjs",
                hidden_act,
                chosen_grads[partition_key],
                preferred_element_type=jnp.float32,
            ).reshape(hidden_width, 2 * sub_width)
            for partition_key in range(level_count)
        ]
    )
    down_left_term = jnp.dot(hidden_flat.T, back_down, preferred_element_type=jnp.float32)
    down_right_term = jnp.dot(low_down.T, cotangent, preferred_element_type=jnp.float32)
    grad_down_tiles, grad_down_left, grad_down_right = (
        lax.psum_scatter(
            down_terms.astype(jnp.bfloat16), "tok", scatter_dimension=1, tiled=True
        ).astype(jnp.float32),
        lax.psum_scatter(
            down_left_term.astype(jnp.bfloat16), "tok", scatter_dimension=0, tiled=True
        ).astype(jnp.float32),
        lax.psum_scatter(
            down_right_term.astype(jnp.bfloat16), "tok", scatter_dimension=0, tiled=True
        ).astype(jnp.float32),
    )
    grad_pre = (grad_hidden * slope).astype(jnp.bfloat16)
    grad_flat = grad_pre.reshape(token_rows, hidden_width)
    back_up = lax.psum(
        jnp.dot(grad_flat, up_right.T, preferred_element_type=jnp.float32).astype(jnp.bfloat16),
        "hid",
    )
    in_parts = [
        place(
            jnp.einsum(
                "tbh,jsbh->tbjs",
                grad_pre,
                up_blocks[partition_key],
                preferred_element_type=jnp.float32,
            ),
            partition_key,
        )
        for partition_key in range(level_count)
    ]
    input_acc = in_parts[0].astype(jnp.float32)
    for partition_key in range(1, level_count):
        input_acc = input_acc + partner(in_parts[partition_key], "hid", partition_key - 1).astype(
            jnp.float32
        )
    grad_tokens = (
        input_acc + jnp.dot(back_up, up_left.T, preferred_element_type=jnp.float32)
    ).astype(jnp.bfloat16)
    up_terms = jnp.stack(
        [
            jnp.einsum(
                "tbjs,tbh->jsbh",
                chosen_inputs[partition_key],
                grad_pre,
                preferred_element_type=jnp.float32,
            ).reshape(2 * sub_width, hidden_width)
            for partition_key in range(level_count)
        ]
    )
    up_right_term = jnp.dot(low_up.T, grad_flat, preferred_element_type=jnp.float32)
    up_left_term = jnp.dot(tokens.T, back_up, preferred_element_type=jnp.float32)
    grad_up_tiles, grad_up_right, grad_up_left = (
        lax.psum_scatter(
            up_terms.astype(jnp.bfloat16), "tok", scatter_dimension=1, tiled=True
        ).astype(jnp.float32),
        lax.psum_scatter(
            up_right_term.astype(jnp.bfloat16), "tok", scatter_dimension=0, tiled=True
        ).astype(jnp.float32),
        lax.psum_scatter(
            up_left_term.astype(jnp.bfloat16), "tok", scatter_dimension=0, tiled=True
        ).astype(jnp.float32),
    )
    return (
        layer_out,
        grad_tokens,
        grad_up_tiles.astype(jnp.bfloat16),
        grad_down_tiles.astype(jnp.bfloat16),
        grad_up_left.astype(jnp.bfloat16),
        grad_up_right.astype(jnp.bfloat16),
        grad_down_left.astype(jnp.bfloat16),
        grad_down_right.astype(jnp.bfloat16),
    )


def solution(mesh):
    return jax.shard_map(
        on_device,
        mesh=mesh,
        in_specs=(
            P("tok", "hid"),
            P("tok", "hid"),
            P(None, None, "hid"),
            P(None, "hid", None),
            P(None, "hid", None),
            P("hid", None),
            P(None, "hid"),
            P("hid", None),
            P(None, "hid"),
        ),
        out_specs=(
            P("tok", "hid"),
            P("tok", "hid"),
            P(None, "tok", "hid"),
            P(None, ("hid", "tok"), None),
            P(("hid", "tok"), None),
            P("tok", "hid"),
            P(("hid", "tok"), None),
            P("tok", "hid"),
        ),
        check_vma=False,
    )
```

profile of v0, /device:TPU:0, one launch (start us, length us, event | category | flops | bytes accessed | tf_op | source)
XLA Modules:
  0.0 1066.0 jit_solution(17671803929161802308)
XLA Ops:
  23.9 17.7 %fusion.202 = (bf16[1,3072,1024]{2,1,0:T(8,128)(2,1)}, bf16[1,3072,1024]{2,1,0:T(8,128)(2,1)}, bf16[1,3072,1024]{2,1,0:T(8,128)(2,1)}, bf16[1,3072,1024]{2,1,0:T(8,128)(2,1)}) fusion(bf16[4,3072,1024]{2,1,0:T(8,128)(2,1)} %param.12), kind=kLoop, calls=%fused_computation.185 | loop fusion | bytes 50331648 | tf_op jit(solution)/shard_map/slice | solution.py:49
  41.6 18.0 %fusion.203 = (bf16[1,1024,3072]{2,1,0:T(8,128)(2,1)}, bf16[1,1024,3072]{2,1,0:T(8,128)(2,1)}, bf16[1,1024,3072]{2,1,0:T(8,128)(2,1)}, bf16[1,1024,3072]{2,1,0:T(8,128)(2,1)}) fusion(bf16[4,1024,3072]{2,1,0:T(8,128)(2,1)} %param.11), kind=kLoop, calls=%fused_computation.186 | loop fusion | bytes 50331648 | tf_op jit(solution)/shard_map/slice | solution.py:45
  97.2 12.0 %reshape.137 = bf16[2,512,12,256]{3,2,1,0:T(8,128)(2,1)} reshape(bf16[1,1024,3072]{2,1,0:T(8,128)(2,1)} %get-tuple-element.43) | data formatting | bytes 12582912 | tf_op jit(solution)/shard_map/reshape;squeeze | solution.py:45
  109.3 12.1 %reshape.136 = bf16[2,512,12,256]{3,2,1,0:T(8,128)(2,1)} reshape(bf16[1,1024,3072]{2,1,0:T(8,128)(2,1)} %get-tuple-element.41) | data formatting | bytes 12582912 | tf_op jit(solution)/shard_map/reshape;squeeze | solution.py:45
  121.4 12.0 %reshape.135 = bf16[2,512,12,256]{3,2,1,0:T(8,128)(2,1)} reshape(bf16[1,1024,3072]{2,1,0:T(8,128)(2,1)} %get-tuple-element.40) | data formatting | bytes 12582912 | tf_op jit(solution)/shard_map/reshape;squeeze | solution.py:45
  221.8 18.0 %fusion.32 = f32[12,256,256,1]{1,2,3,0:T(8,128)} fusion(bf16[2,512,12,256]{3,2,1,0:T(8,128)(2,1)} %reshape.138, bf16[256,12,2,512]{3,1,0,2:T(8,128)(2,1)} %convert_bitcast_fusion.4), kind=kOutput, calls=%fused_computation.48 | convolution fusion | flops 1610612736 | bytes 15728640 | tf_op jit(solution)/shard_map/tbjs,jsbh->tbh/dot_general | solution.py:84
  239.9 18.2 %fusion.36 = f32[12,256,256,1]{1,2,3,0:T(8,128)} fusion(bf16[2,512,12,256]{3,2,1,0:T(8,128)(2,1)} %reshape.137, bf16[256,12,2,512]{3,1,0,2:T(8,128)(2,1)} %convert_bitcast_fusion.5), kind=kOutput, calls=%fused_computation.52 | convolution fusion | flops 1610612736 | bytes 15728640 | tf_op jit(solution)/shard_map/tbjs,jsbh->tbh/dot_general | solution.py:84
  258.1 18.4 %fusion.40 = f32[12,256,256,1]{1,2,3,0:T(8,128)} fusion(bf16[2,512,12,256]{3,2,1,0:T(8,128)(2,1)} %reshape.136, bf16[256,12,2,512]{3,1,0,2:T(8,128)(2,1)} %convert_bitcast_fusion.6), kind=kOutput, calls=%fused_computation.56 | convolution fusion | flops 1610612736 | bytes 15728640 | tf_op jit(solution)/shard_map/tbjs,jsbh->tbh/dot_general | solution.py:84
  310.3 24.7 %multiply_convert_fusion = (bf16[256,12,256]{0,2,1:T(8,128)(2,1)S(1)}, f32[256,12,256]{0,2,1:T(8,128)}) fusion(f32[12,256,256,1]{1,2,3,0:T(8,128)} %fusion.32, f32[12,256,256,1]{1,2,3,0:T(8,128)} %fusion.36, f32[12,256,256,1]{1,2,3,0:T(8,128)} %fusion.40, f32[256,12,256]{0,2,1:T(8,128)} %bitcast.329, bf16[2,512,12,256]{3,2,1,0:T(8,128)(2,1)} %reshape.135, ...), kind=kOutput, calls=%fused_computation.117 | convolution fusion | flops 1620836352 | bytes 29884416 | tf_op jit(solution)/shard_map/tbjs,jsbh->tbh/dot_general | solution.py:84
  334.9 19.7 %fusion.122 = bf16[256,12,256]{0,2,1:T(8,128)(2,1)} fusion(f32[256,12,256]{0,2,1:T(8,128)} %get-tuple-element.51, f32[12,256,256,1]{1,2,3,0:T(8,128)} %fusion.16, f32[12,256,256,1]{1,2,3,0:T(8,128)} %fusion.20, f32[12,256,256,1]{1,2,3,0:T(8,128)} %fusion.24, f32[256,12,256]{0,2,1:T(8,128)} %bitcast.339, bf16[12,256,2,512]{3,2,1,0:T(2,128)(2,1)} %reshape_squeeze.28, ...), kind=kOutput, calls=%fused_computation.108 | convolution fusion | flops 1628700672 | bytes 29884416 | tf_op jit(solution)/shard_map/tbjs,bhjs->tbh/dot_general | solution.py:131
  354.7 14.3 %convert_bitcast_fusion.8 = bf16[2,512,12,256]{1,3,0,2:T(8,128)(2,1)} fusion(bf16[256,12,2,512]{3,1,0,2:T(8,128)(2,1)} %convert_bitcast_fusion.4, bf16[256,12,256]{0,2,1:T(8,128)(2,1)} %fusion.122), kind=kOutput, calls=%fused_computation.26 | convolution fusion | flops 1613758464 | bytes 14155776 | tf_op jit(solution)/shard_map/tbjs,tbh->jsbh/dot_general | solution.py:189
  369.0 14.1 %convert_bitcast_fusion.9 = bf16[2,512,12,256]{1,3,0,2:T(8,128)(2,1)} fusion(bf16[256,12,2,512]{3,1,0,2:T(8,128)(2,1)} %convert_bitcast_fusion.5, bf16[256,12,256]{0,2,1:T(8,128)(2,1)S(1)} %copy-done.2), kind=kOutput, calls=%fused_computation.27 | convolution fusion | flops 1613758464 | bytes 14155776 | tf_op jit(solution)/shard_map/tbjs,tbh->jsbh/dot_general | solution.py:189
  383.1 13.9 %convert_bitcast_fusion.10 = bf16[2,512,12,256]{1,3,0,2:T(8,128)(2,1)} fusion(bf16[256,12,2,512]{3,1,0,2:T(8,128)(2,1)} %convert_bitcast_fusion.6, bf16[256,12,256]{0,2,1:T(8,128)(2,1)S(1)} %copy-done.2), kind=kOutput, calls=%fused_computation.28 | convolution fusion | flops 1613758464 | bytes 14155776 | tf_op jit(solution)/shard_map/tbjs,tbh->jsbh/dot_general | solution.py:189
  410.0 12.6 %copy.229 = bf16[2,512,12,256]{1,0,3,2:T(2,128)(2,1)} copy(bf16[2,512,12,256]{1,3,0,2:T(8,128)(2,1)} %convert_bitcast_fusion.8) | data formatting | bytes 12582912 | tf_op jit(solution)/shard_map/tbjs,tbh->jsbh/transpose | solution.py:189
  433.5 12.6 %copy.227 = bf16[2,512,12,256]{1,0,3,2:T(2,128)(2,1)} copy(bf16[2,512,12,256]{1,3,0,2:T(8,128)(2,1)} %convert_bitcast_fusion.9) | data formatting | bytes 12582912 | tf_op jit(solution)/shard_map/tbjs,tbh->jsbh/transpose | solution.py:189
  457.1 12.6 %copy.225 = bf16[2,512,12,256]{1,0,3,2:T(2,128)(2,1)} copy(bf16[2,512,12,256]{1,3,0,2:T(8,128)(2,1)} %convert_bitcast_fusion.10) | data formatting | bytes 12582912 | tf_op jit(solution)/shard_map/tbjs,tbh->jsbh/transpose | solution.py:189
  480.7 12.9 %copy.223 = bf16[2,512,12,256]{1,0,3,2:T(2,128)(2,1)} copy(bf16[2,512,12,256]{1,3,0,2:T(8,128)(2,1)} %convert_bitcast_fusion.11) | data formatting | bytes 12582912 | tf_op jit(solution)/shard_map/tbjs,tbh->jsbh/transpose | solution.py:189
  504.7 20.7 %pad_maximum_fusion = bf16[4,1024,3072]{1,2,0:T(8,128)(2,1)} fusion(bf16[1,1024,3072]{1,2,0:T(8,128)(2,1)} %stack_reshape.35, bf16[1,1024,3072]{1,2,0:T(8,128)(2,1)} %stack_reshape.34, bf16[1,1024,3072]{1,2,0:T(8,128)(2,1)} %stack_reshape.33, bf16[1,1024,3072]{1,2,0:T(8,128)(2,1)} %stack_reshape.32), kind=kLoop, calls=%fused_computation | loop fusion | flops 37748736 | bytes 50331648 | tf_op jit(solution)/shard_map/stack | solution.py:187
  525.5 51.7 %all-reduce.5.cloned.1.call-done = (bf16[256,256]{1,0:T(8,128)(2,1)}, bf16[256,256]{1,0:T(8,128)(2,1)}) async-done(((bf16[256,256]{1,0:T(8,128)(2,1)}, bf16[256,256]{1,0:T(8,128)(2,1)}), (bf16[256,256]{1,0:T(8,128)(2,1)}, bf16[256,256]{1,0:T(8,128)(2,1)})) %all-reduce.5.cloned.1.call-update) | async-done | bytes 262160 | tf_op jit(solution)/shard_map/psum | solution.py:93
  586.5 13.0 %fusion.113 = bf16[12,256,2,512]{3,1,2,0:T(8,128)(2,1)S(1)} fusion(bf16[256,12,2,512]{3,1,0,2:T(8,128)(2,1)} %convert_bitcast_fusion, bf16[256,12,256]{0,2,1:T(8,128)(2,1)S(1)} %get-tuple-element.50), kind=kOutput, calls=%fused_computation.101 | convolution fusion | flops 1613758464 | bytes 14155776 | tf_op jit(solution)/shard_map/tbh,tbjs->bhjs/dot_general | solution.py:139
  704.2 21.0 %pad_maximum_fusion.1 = bf16[4,3072,1024]{2,1,0:T(8,128)(2,1)} fusion(bf16[1,3072,1024]{2,1,0:T(8,128)(2,1)} %stack_reshape.39, bf16[1,3072,1024]{2,1,0:T(8,128)(2,1)} %stack_reshape.38, bf16[1,3072,1024]{2,1,0:T(8,128)(2,1)} %stack_reshape.37, bf16[1,3072,1024]{2,1,0:T(8,128)(2,1)} %stack_reshape.36), kind=kLoop, calls=%fused_computation.1 | loop fusion | flops 37748736 | bytes 50331648 | tf_op jit(solution)/shard_map/stack | solution.py:137
  730.3 13.0 %fusion.174 = bf16[256,3,512]{2,1,0:T(4,128)(2,1)} fusion(f32[256,12,2,512]{3,0,2,1:T(8,128)S(1)} %fusion.93, pred[4,12,2,3]{1,3,2,0:T(4,128)(4,1)S(1)} %copy-done.15), kind=kOutput, calls=%fused_computation.151 | convolution fusion | flops 113639424 | bytes 13370368 | tf_op jit(solution)/shard_map/kdow,dog->kgw/dot_general | solution.py:63
  754.0 13.2 %fusion.171 = bf16[256,3,512]{2,1,0:T(4,128)(2,1)} fusion(f32[256,12,2,512]{3,0,2,1:T(8,128)S(1)} %fusion.90, pred[4,12,2,3]{1,3,2,0:T(4,128)(4,1)S(1)} %copy-done.15), kind=kOutput, calls=%fused_computation.150 | convolution fusion | flops 113639424 | bytes 13370368 | tf_op jit(solution)/shard_map/kdow,dog->kgw/dot_general | solution.py:63
  776.8 13.5 %convert_bitcast_fusion.13 = f32[256,3,512]{2,1,0:T(4,128)} fusion(f32[256,12,2,512]{3,0,2,1:T(8,128)S(1)} %fusion.84, pred[4,12,2,3]{1,3,2,0:T(4,128)(4,1)S(1)} %copy-done.15), kind=kOutput, calls=%fused_computation.130 | convolution fusion | flops 114032640 | bytes 14156800 | tf_op jit(solution)/shard_map/kdow,dog->kgw/dot_general | solution.py:63
  800.7 12.4 %fusion.168 = bf16[256,3,512]{2,1,0:T(4,128)(2,1)S(1)} fusion(f32[256,12,2,512]{3,0,2,1:T(8,128)S(1)} %fusion.87, pred[4,12,2,3]{1,3,2,0:T(4,128)(4,1)S(1)} %copy-done.15), kind=kOutput, calls=%fused_computation.149 | convolution fusion | flops 113639424 | bytes 13370368 | tf_op jit(solution)/shard_map/kdow,dog->kgw/dot_general | solution.py:63
  824.0 12.5 %fusion.183 = bf16[256,3,512]{2,1,0:T(4,128)(2,1)S(1)} fusion(f32[256,12,2,512]{3,0,2,1:T(8,128)S(1)} %fusion.81, pred[4,12,2,3]{1,3,2,0:T(4,128)(4,1)S(1)} %copy-done.15), kind=kOutput, calls=%fused_computation.154 | convolution fusion | flops 113639424 | bytes 13370368 | tf_op jit(solution)/shard_map/kdow,dog->kgw/dot_general | solution.py:63
  848.8 12.3 %fusion.72 = f32[256,12,2,512]{3,0,2,1:T(8,128)} fusion(bf16[2,512,12,256]{3,2,1,0:T(8,128)(2,1)} %reshape.135, bf16[256,12,256]{0,2,1:T(8,128)(2,1)S(1)} %copy-done.3), kind=kOutput, calls=%fused_computation.88 | convolution fusion | flops 1610612736 | bytes 20447232 | tf_op jit(solution)/shard_map/tbh,jsbh->tbjs/dot_general | solution.py:169
  861.0 12.7 %fusion.75 = f32[256,12,2,512]{3,0,2,1:T(8,128)} fusion(bf16[2,512,12,256]{3,2,1,0:T(8,128)(2,1)} %reshape.136, bf16[256,12,256]{0,2,1:T(8,128)(2,1)S(1)} %copy-done.3), kind=kOutput, calls=%fused_computation.89 | convolution fusion | flops 1610612736 | bytes 20447232 | tf_op jit(solution)/shard_map/tbh,jsbh->tbjs/dot_general | solution.py:169
  873.8 12.3 %fusion.180 = bf16[256,3,512]{2,1,0:T(4,128)(2,1)S(1)} fusion(f32[256,12,2,512]{3,0,2,1:T(8,128)S(1)} %fusion.78, pred[4,12,2,3]{1,3,2,0:T(4,128)(4,1)S(1)} %copy-done.15), kind=kOutput, calls=%fused_computation.153 | convolution fusion | flops 113639424 | bytes 13370368 | tf_op jit(solution)/shard_map/kdow,dog->kgw/dot_general | solution.py:63
  888.1 19.2 %fusion.177 = bf16[256,3,512]{2,1,0:T(4,128)(2,1)S(1)} fusion(f32[256,12,2,512]{3,0,2,1:T(8,128)} %fusion.75, pred[4,12,2,3]{1,3,2,0:T(4,128)(4,1)S(1)} %copy-done.15), kind=kOutput, calls=%fused_computation.152 | convolution fusion | flops 113639424 | bytes 13370368 | tf_op jit(solution)/shard_map/kdow,dog->kgw/dot_general | solution.py:63
  910.7 18.9 %convert_bitcast_fusion.12 = f32[256,3,512]{2,1,0:T(4,128)} fusion(f32[256,12,2,512]{3,0,2,1:T(8,128)} %fusion.72, pred[4,12,2,3]{1,3,2,0:T(4,128)(4,1)S(1)} %copy-done.15), kind=kOutput, calls=%fused_computation.129 | convolution fusion | flops 114032640 | bytes 14156800 | tf_op jit(solution)/shard_map/kdow,dog->kgw/dot_general | solution.py:63
  948.8 109.9 %reduce-scatter.11.cloned.1.call-done = bf16[4,768,1024]{2,1,0:T(8,128)(2,1)} async-done(((bf16[4,3072,1024]{2,1,0:T(8,128)(2,1)}), bf16[4,768,1024]{2,1,0:T(8,128)(2,1)}) %reduce-scatter.11.cloned.1.call-update) | async-done | bytes 6291472 | tf_op jit(solution)/shard_map/reduce_scatter | solution.py:151
  (169 shorter events, 430.9 us)
Async XLA Ops:
  7.2 163.6 %copy-start = (bf16[3072,256]{1,0:T(8,128)(2,1)S(1)}, bf16[3072,256]{1,0:T(8,128)(2,1)}, u32[]{:S(2)}) copy-start(bf16[3072,256]{1,0:T(8,128)(2,1)} %param.16) | copy-start | bytes 4718596
  7.2 159.6 %all-reduce.7.cloned.1.call-start = ((), (), s32[]{:S(2)}) async-start(), calls=%async_computation.13 | async-start | bytes 524288 | tf_op jit(solution)/shard_map/psum | solution.py:74
  9.6 164.3 %collective-permute-start.2 = (bf16[256,1536]{0,1:T(8,128)(2,1)}, bf16[256,1536]{0,1:T(8,128)(2,1)}, u32[]{:S(2)}, u32[]{:S(2)}) collective-permute-start(bf16[256,1536]{0,1:T(8,128)(2,1)} %copy.134), channel_id=1, source_target_pairs={{0,16},{16,0},{4,20},{20,4},{8,24},{24,8},{12,28},{28,12},{1,17},{... | collective-permute-start | bytes 2359304 | tf_op jit(solution)/shard_map/ppermute | solution.py:17
  13.7 163.1 %collective-permute-start.1 = (bf16[256,1536]{0,1:T(8,128)(2,1)}, bf16[256,1536]{0,1:T(8,128)(2,1)}, u32[]{:S(2)}, u32[]{:S(2)}) collective-permute-start(bf16[256,1536]{0,1:T(8,128)(2,1)} %copy.134), channel_id=1, source_target_pairs={{0,8},{8,0},{4,12},{12,4},{16,24},{24,16},{20,28},{28,20},{1,9},{9... | collective-permute-start | bytes 2359304 | tf_op jit(solution)/shard_map/ppermute | solution.py:17
  15.2 164.1 %collective-permute-start = (bf16[256,1536]{0,1:T(8,128)(2,1)}, bf16[256,1536]{0,1:T(8,128)(2,1)}, u32[]{:S(2)}, u32[]{:S(2)}) collective-permute-start(bf16[256,1536]{0,1:T(8,128)(2,1)} %copy.134), channel_id=1, source_target_pairs={{0,4},{4,0},{8,12},{12,8},{16,20},{20,16},{24,28},{28,24},{1,5},{5... | collective-permute-start | bytes 2359304 | tf_op jit(solution)/shard_map/ppermute | solution.py:17
  18.1 163.0 %collective-permute-start.8 = (bf16[256,1536]{0,1:T(8,128)(2,1)S(1)}, bf16[256,1536]{0,1:T(8,128)(2,1)}, u32[]{:S(2)}, u32[]{:S(2)}) collective-permute-start(bf16[256,1536]{0,1:T(8,128)(2,1)S(1)} %copy.182), channel_id=1, source_target_pairs={{0,16},{16,0},{4,20},{20,4},{8,24},{24,8},{12,28},{28,12},{1,17},{... | collective-permute-start | bytes 2359304 | tf_op jit(solution)/shard_map/ppermute | solution.py:17
  18.5 176.7 %collective-permute-start.7 = (bf16[256,1536]{0,1:T(8,128)(2,1)S(1)}, bf16[256,1536]{0,1:T(8,128)(2,1)}, u32[]{:S(2)}, u32[]{:S(2)}) collective-permute-start(bf16[256,1536]{0,1:T(8,128)(2,1)S(1)} %copy.182), channel_id=1, source_target_pairs={{0,8},{8,0},{4,12},{12,4},{16,24},{24,16},{20,28},{28,20},{1,9},{9... | collective-permute-start | bytes 2359304 | tf_op jit(solution)/shard_map/ppermute | solution.py:17
  23.8 553.4 %all-reduce.5.cloned.1.call-start = ((), (), s32[]{:S(2)}) async-start(), calls=%async_computation.12 | async-start | bytes 524288 | tf_op jit(solution)/shard_map/psum | solution.py:93
  41.6 18.0 %copy-start.16 = (s32[4,12,2]{1,2,0:T(2,128)S(1)}, s32[4,12,2]{1,2,0:T(2,128)}, u32[]{:S(2)}) copy-start(s32[4,12,2]{1,2,0:T(2,128)} %param.13) | copy-start | bytes 1156
  173.9 35.0 %collective-permute-start.6 = (bf16[256,1536]{0,1:T(8,128)(2,1)S(1)}, bf16[256,1536]{0,1:T(8,128)(2,1)}, u32[]{:S(2)}, u32[]{:S(2)}) collective-permute-start(bf16[256,1536]{0,1:T(8,128)(2,1)S(1)} %copy.182), channel_id=1, source_target_pairs={{0,4},{4,0},{8,12},{12,8},{16,20},{20,16},{24,28},{28,24},{1,5},{5... | collective-permute-start | bytes 2359304 | tf_op jit(solution)/shard_map/ppermute | solution.py:17
  183.8 6.3 copy-start.6
  354.7 14.3 %copy-start.2 = (bf16[256,12,256]{0,2,1:T(8,128)(2,1)S(1)}, bf16[256,12,256]{0,2,1:T(8,128)(2,1)}, u32[]{:S(2)}) copy-start(bf16[256,12,256]{0,2,1:T(8,128)(2,1)} %fusion.122) | copy-start | bytes 4718596
  369.0 28.0 %slice-start = ((s8[8388608]{0:T(1024)(128)(4,1)}), s8[4194304]{0:T(1024)(128)(4,1)S(1)}, s32[]{:S(2)}) async-start(s8[8388608]{0:T(1024)(128)(4,1)} %bitcast.327), calls=%async_computation.14 | async-start | bytes 8388608
  383.1 13.9 %slice-start.1 = ((s8[8388608]{0:T(1024)(128)(4,1)}), s8[4194304]{0:T(1024)(128)(4,1)S(1)}, s32[]{:S(2)}) async-start(s8[8388608]{0:T(1024)(128)(4,1)} %bitcast.327), calls=%async_computation.15 | async-start | bytes 8388608
  397.0 11.8 %copy-start.10 = (bf16[256,3072]{1,0:T(8,128)(2,1)S(1)}, bf16[256,3072]{1,0:T(8,128)(2,1)}, u32[]{:S(2)}) copy-start(bf16[256,3072]{1,0:T(8,128)(2,1)} %param.15) | copy-start | bytes 4718596
  504.7 435.4 %reduce-scatter.9.cloned.1.call-start = ((), (), s32[]{:S(2)}) async-start(), calls=%async_computation.6 | async-start | bytes 31457280 | tf_op jit(solution)/shard_map/reduce_scatter | solution.py:201
  525.4 59.2 %copy-start.3 = (bf16[256,12,256]{0,2,1:T(8,128)(2,1)S(1)}, bf16[256,12,256]{0,2,1:T(8,128)(2,1)}, u32[]{:S(2)}) copy-start(bf16[256,12,256]{0,2,1:T(8,128)(2,1)} %fusion.122) | copy-start | bytes 4718596
  525.4 59.2 %copy-start.12 = (bf16[256,256]{1,0:T(8,128)(2,1)S(1)}, bf16[256,256]{1,0:T(8,128)(2,1)}, u32[]{:S(2)}) copy-start(bf16[256,256]{1,0:T(8,128)(2,1)} %get-tuple-element.34) | copy-start | bytes 393220
  525.4 423.4 %reduce-scatter.19.cloned.1.call-start = ((), (), s32[]{:S(2)}) async-start(), calls=%async_computation.11 | async-start | bytes 983040
  582.0 366.8 %reduce-scatter.17.cloned.1.call-start = ((), (), s32[]{:S(2)}) async-start(), calls=%async_computation.10 | async-start | bytes 983040 | tf_op jit(solution)/shard_map/reduce_scatter | solution.py:157
  584.6 364.3 %reduce-scatter.13.cloned.1.call-start = ((), (), s32[]{:S(2)}) async-start(), calls=%async_computation.8 | async-start | bytes 1966080 | tf_op jit(solution)/shard_map/reduce_scatter | solution.py:204
  586.4 362.4 %reduce-scatter.15.cloned.1.call-start = ((), (), s32[]{:S(2)}) async-start(), calls=%async_computation.9 | async-start | bytes 1966080 | tf_op jit(solution)/shard_map/reduce_scatter | solution.py:154
  691.2 11.2 %copy-start.11 = (bf16[256,256]{1,0:T(8,128)(2,1)S(1)}, bf16[256,256]{1,0:T(8,128)(2,1)}, u32[]{:S(2)}) copy-start(bf16[256,256]{1,0:T(8,128)(2,1)} %get-tuple-element.35) | copy-start | bytes 393220
  704.1 354.6 %reduce-scatter.11.cloned.1.call-start = ((), (), s32[]{:S(2)}) async-start(), calls=%async_computation.7 | async-start | bytes 31457280 | tf_op jit(solution)/shard_map/reduce_scatter | solution.py:151
  747.8 161.3 %collective-permute-start.5 = (bf16[256,1536]{1,0:T(8,128)(2,1)}, bf16[256,1536]{1,0:T(8,128)(2,1)}, u32[]{:S(2)}, u32[]{:S(2)}) collective-permute-start(bf16[256,1536]{1,0:T(8,128)(2,1)} %copy.180), channel_id=1, source_target_pairs={{0,16},{16,0},{4,20},{20,4},{8,24},{24,8},{12,28},{28,12},{1,17},{... | collective-permute-start | bytes 2359304 | tf_op jit(solution)/shard_map/ppermute | solution.py:17
  771.9 161.3 %collective-permute-start.4 = (bf16[256,1536]{1,0:T(8,128)(2,1)}, bf16[256,1536]{1,0:T(8,128)(2,1)}, u32[]{:S(2)}, u32[]{:S(2)}) collective-permute-start(bf16[256,1536]{1,0:T(8,128)(2,1)} %copy.175), channel_id=1, source_target_pairs={{0,8},{8,0},{4,12},{12,4},{16,24},{24,16},{20,28},{28,20},{1,9},{9... | collective-permute-start | bytes 2359304 | tf_op jit(solution)/shard_map/ppermute | solution.py:17
  815.0 118.2 %collective-permute-start.3 = (bf16[256,1536]{1,0:T(8,128)(2,1)}, bf16[256,1536]{1,0:T(8,128)(2,1)}, u32[]{:S(2)}, u32[]{:S(2)}) collective-permute-start(bf16[256,1536]{1,0:T(8,128)(2,1)} %copy.169), channel_id=1, source_target_pairs={{0,4},{4,0},{8,12},{12,8},{16,20},{20,16},{24,28},{28,24},{1,5},{5... | collective-permute-start | bytes 2359304 | tf_op jit(solution)/shard_map/ppermute | solution.py:17
  838.9 97.7 %collective-permute-start.11 = (bf16[256,1536]{1,0:T(8,128)(2,1)}, bf16[256,1536]{1,0:T(8,128)(2,1)}, u32[]{:S(2)}, u32[]{:S(2)}) collective-permute-start(bf16[256,1536]{1,0:T(8,128)(2,1)} %copy.221), channel_id=1, source_target_pairs={{0,16},{16,0},{4,20},{20,4},{8,24},{24,8},{12,28},{28,12},{1,17},{... | collective-permute-start | bytes 2359304 | tf_op jit(solution)/shard_map/ppermute | solution.py:17
  887.9 48.7 %collective-permute-start.10 = (bf16[256,1536]{1,0:T(8,128)(2,1)}, bf16[256,1536]{1,0:T(8,128)(2,1)}, u32[]{:S(2)}, u32[]{:S(2)}) collective-permute-start(bf16[256,1536]{1,0:T(8,128)(2,1)} %copy.216), channel_id=1, source_target_pairs={{0,8},{8,0},{4,12},{12,4},{16,24},{24,16},{20,28},{28,20},{1,9},{9... | collective-permute-start | bytes 2359304 | tf_op jit(solution)/shard_map/ppermute | solution.py:17
  909.2 27.4 %collective-permute-start.9 = (bf16[256,1536]{1,0:T(8,128)(2,1)}, bf16[256,1536]{1,0:T(8,128)(2,1)}, u32[]{:S(2)}, u32[]{:S(2)}) collective-permute-start(bf16[256,1536]{1,0:T(8,128)(2,1)} %copy.210), channel_id=1, source_target_pairs={{0,4},{4,0},{8,12},{12,8},{16,20},{20,16},{24,28},{28,24},{1,5},{5... | collective-permute-start | bytes 2359304 | tf_op jit(solution)/shard_map/ppermute | solution.py:17
  929.6 7.0 copy-start.13
  936.6 122.1 %copy-start.1 = (bf16[3072,256]{1,0:T(8,128)(2,1)S(1)}, bf16[3072,256]{1,0:T(8,128)(2,1)}, u32[]{:S(2)}) copy-start(bf16[3072,256]{1,0:T(8,128)(2,1)} %param.16) | copy-start | bytes 4718596
  (7 other events, 32.0 us)
Sparse Core Ops, SparseCore 0:
  24.0 106.4 all-reduce.6
  504.8 72.3 all-reduce.4
  579.8 179.7 reduce-scatter.8
  762.7 23.2 reduce-scatter.18
  789.0 23.2 reduce-scatter.16
  815.4 28.1 reduce-scatter.12
  846.8 28.1 reduce-scatter.14
  878.3 180.4 reduce-scatter.10
where the time goes:
time: 1080 us; the launch traced here: 1070 us
  matrix products  480 us (44%)
  local copies, waits for them, and re-layouts  352 us (33%)
  waiting for transfers between devices  162 us (15%)
  other arithmetic  42.3 us (4%)
  starting transfers between devices  15.1 us (1%)
  between operations  14.9 us (1%)
    dot_general x8, matrix products, place(): jnp.einsum('kdow,dog->kgw', partner_pairs, select_float_values[partition_...  115 us
    reduce_scatter x1, waiting for transfers between devices, on_device(): lax.psum_scatter(down_terms.astype(jnp.bfloat16), 'tok', scatter_dimensio...  110 us
    dot_general x4, matrix products, on_device(): jnp.einsum('tbjs,jsbh->tbh', chosen_inputs[partition_key], up_blocks[part...  79.3 us
    dot_general x4, matrix products, on_device(): jnp.einsum('tbjs,bhjs->tbh', chosen_grads[partition_key], down_blocks[par...  53.5 us
    dot_general x4, matrix products, on_device(): jnp.einsum('tbjs,tbh->jsbh', chosen_inputs[partition_key], grad_pre, pref...  52.8 us
    psum x1, waiting for transfers between devices, on_device(): lax.psum(jnp.dot(hidden_flat, down_left, preferred_element_type=jnp.float...  51.7 us
    transpose x4, local copies, waits for them, and re-layouts, on_device(): jnp.einsum('tbjs,tbh->jsbh', chosen_inputs[partition_key], grad_pre, pref...  50.6 us
    another operation x4, local copies, waits for them, and re-layouts, on_device(): up_tiles[partition_key].reshape(2, sub_width, block_count, block_width)  48.2 us
  transfers between devices with their start and end apart: 20, of which 2 were waited for; matrix products, arithmetic and copies ran while one was open for 54% of the time, Pallas kernels for 0%

commit v1 on v0

v1 whole, which is shorter than its diff:
```python
import functools
import math

import jax
import jax.numpy as jnp
from jax import lax
from jax.experimental import pallas as pl
from jax.experimental.pallas import tpu as pltpu
from jax.sharding import PartitionSpec as P

GELU_SCALE = 0.7978845608028654
GELU_CUBIC = 0.044715
F32 = jnp.float32
BF16 = jnp.bfloat16
WHOLE = pl.BlockSpec(memory_space=pltpu.VMEM)
VMEM_LIMIT = 56 * 1024 * 1024


def swap(block, axis, mask):
    count = lax.axis_size(axis)
    return lax.ppermute(block, axis, [(i, i ^ mask) for i in range(count)])


def gather_list(block):
    count = lax.axis_size("tok")
    items = {0: block}
    bit = count // 2
    while bit:
        for mask in list(items):
            items[mask | bit] = swap(items[mask], "tok", bit)
        bit //= 2
    return [items[d] for d in range(count)]


def exchange_list(pick):
    me = lax.axis_index("tok")
    return [pick(me)] + [
        swap(pick(me ^ d), "tok", d) for d in range(1, lax.axis_size("tok"))
    ]


def gelu_parts(pre_act):
    inner = GELU_SCALE * (pre_act + GELU_CUBIC * pre_act * pre_act * pre_act)
    tanh_value = jnp.tanh(inner)
    value = 0.5 * pre_act * (1.0 + tanh_value)
    slope = 0.5 * (1.0 + tanh_value) + 0.5 * pre_act * (
        1.0 - tanh_value * tanh_value
    ) * GELU_SCALE * (1.0 + 3.0 * GELU_CUBIC * pre_act * pre_act)
    return (value, slope)


def dot_nn(a, b):
    return jnp.dot(a, b, preferred_element_type=F32)


def dot_nt(a, b):
    return lax.dot_general(a, b, (((1,), (1,)), ((), ())), preferred_element_type=F32)


def split_kernel(levels, parts, sub, *refs):
    feats, (out, own_t) = refs[:levels], refs[levels:]
    width = sub // parts
    for k in range(levels):
        for c in range(3):
            turned = feats[k][:, c * sub : (c + 1) * sub].T
            for p in range(parts):
                out[p, k * 3 + c] = turned[p * width : (p + 1) * width]
            if k == 0:
                own_t[c * sub : (c + 1) * sub, :] = turned


def block_kernel(levels, sub, steps, index, *refs):
    feats, refs = refs[:levels], refs[levels:]
    grads, refs = refs[:levels], refs[levels:]
    low_up, back_down, up, down, up_right, down_left = refs[:6]
    hid_t, grad_pre_out, out_parts, in_parts, low_down, back_up = refs[6:12]
    out_acc, in_acc, low_acc, back_acc = refs[12:]
    b = pl.program_id(0)

    @pl.when(b == 0)
    def _():
        out_acc[...] = jnp.zeros_like(out_acc)
        in_acc[...] = jnp.zeros_like(in_acc)
        low_acc[...] = jnp.zeros_like(low_acc)
        back_acc[...] = jnp.zeros_like(back_acc)

    pre = dot_nn(low_up[...], up_right[...])
    grad = dot_nt(back_down[...], down_left[...])
    pairs = [(k, j) for k in range(levels) for j in range(2)]
    picks = {(k, j): index[(k * steps + b) * 2 + j] for k, j in pairs}
    for k, j in pairs:
        cols = pl.ds(pl.multiple_of(picks[k, j] * sub, sub), sub)
        pre += dot_nn(feats[k][:, cols], up[k, j * sub : (j + 1) * sub, :])
        grad += dot_nt(grads[k][:, cols], down[k, :, j * sub : (j + 1) * sub])
    value, slope = gelu_parts(pre)
    hidden = value.astype(BF16)
    grad_pre = (grad * slope).astype(BF16)
    hid_t[...] = hidden.T
    grad_pre_out[...] = grad_pre
    low_acc[...] += dot_nn(hidden, down_left[...])
    back_acc[...] += dot_nt(grad_pre, up_right[...])
    for k, j in pairs:
        spot = k * 3 + picks[k, j]
        out_acc[spot] += dot_nn(hidden, down[k, :, j * sub : (j + 1) * sub])
        in_acc[spot] += dot_nt(grad_pre, up[k, j * sub : (j + 1) * sub, :])

    @pl.when(b == steps - 1)
    def _():
        for k in range(levels):
            for c in range(3):
                out_parts[k, :, c * sub : (c + 1) * sub] = out_acc[k * 3 + c].astype(BF16)
                in_parts[k, :, c * sub : (c + 1) * sub] = in_acc[k * 3 + c].astype(BF16)
        low_down[...] = low_acc[...].astype(BF16)
        back_up[...] = back_acc[...].astype(BF16)


def down_kernel(levels, sub, groups, blocks, rows, block_width, index, *refs):
    hid, refs = refs[:groups], refs[groups:]
    grads, refs = refs[:groups], refs[groups:]
    backs, (out, out_left) = refs[:groups], refs[groups:]
    i = pl.program_id(0)
    block = (index[levels * blocks * 2] * (pl.num_programs(0) * rows) + i * rows) // block_width
    lhs = [hid[d][...] for d in range(groups)]
    out_left[...] = sum(dot_nn(lhs[d], backs[d][...]) for d in range(groups)).astype(BF16)
    for k in range(levels):
        for j in range(2):
            pick = index[(k * blocks + block) * 2 + j]
            cols = pl.ds(pl.multiple_of(pick * sub, sub), sub)
            total = sum(dot_nn(lhs[d], grads[d][k, :, cols]) for d in range(groups))
            out[k, :, j * sub : (j + 1) * sub] = total.astype(BF16)


def up_kernel(levels, groups, blocks, index, *refs):
    feats, refs = refs[:groups], refs[groups:]
    grads, refs = refs[:groups], refs[groups:]
    lows, (out, out_right) = refs[:groups], refs[groups:]
    b = pl.program_id(0)
    side = index[levels * blocks * 2] // (groups // 2)
    rhs = [grads[d][...] for d in range(groups)]
    out_right[...] = sum(dot_nn(lows[d][...], rhs[d]) for d in range(groups)).astype(BF16)
    for k in range(levels):
        pick = k * 3 + index[(k * blocks + b) * 2 + side]
        total = sum(dot_nn(feats[d][pick], rhs[d]) for d in range(groups))
        out[k] = total.astype(BF16)


def cost(flops, nbytes):
    return pl.CostEstimate(flops=flops, bytes_accessed=nbytes, transcendentals=0)


def on_device(
    tokens, cotangent, up_tiles, down_tiles, block_index, up_left, up_right, down_left, down_right
):
    hid_count = lax.axis_size("hid")
    groups = lax.axis_size("tok")
    me = lax.axis_index("tok")
    levels = hid_count.bit_length()
    rows, feat = tokens.shape
    sub = feat // 3
    blocks = block_index.shape[1]
    hidden = up_tiles.shape[2]
    width = hidden // blocks
    rank = up_left.shape[1]
    parts = groups // 2
    part = sub // parts
    own = hidden // groups
    own_feat = feat // groups
    own_rank = rank // groups
    index = jnp.concatenate([block_index.reshape(-1), me.astype(jnp.int32).reshape(1)])
    params = pltpu.CompilerParams(
        vmem_limit_bytes=VMEM_LIMIT, dimension_semantics=("arbitrary",)
    )
    sds = jax.ShapeDtypeStruct

    lows = lax.psum(
        (dot_nn(tokens, up_left).astype(BF16), dot_nt(cotangent, down_right).astype(BF16)), "hid"
    )
    low_up, back_down = lows
    feats = [tokens] + [swap(tokens, "hid", 1 << k) for k in range(levels - 1)]
    grads = [cotangent] + [swap(cotangent, "hid", 1 << k) for k in range(levels - 1)]

    split, own_t = pl.pallas_call(
        functools.partial(split_kernel, levels, parts, sub),
        out_shape=(sds((parts, levels * 3, part, rows), BF16), sds((feat, rows), BF16)),
        in_specs=[WHOLE] * levels,
        out_specs=(WHOLE, WHOLE),
        compiler_params=pltpu.CompilerParams(vmem_limit_bytes=VMEM_LIMIT),
        cost_estimate=cost(0, 4 * levels * rows * feat),
    )(*feats)
    feat_items = exchange_list(
        lambda q: lax.dynamic_index_in_dim(split, q % parts, 0, keepdims=False)
    )
    own_items = exchange_list(
        lambda q: lax.dynamic_slice_in_dim(own_t, q * own_feat, own_feat, 0)
    )
    grad_items = gather_list(jnp.stack(grads))
    low_up_items = exchange_list(
        lambda q: lax.dynamic_slice_in_dim(low_up.T, q * own_rank, own_rank, 0)
    )
    back_down_items = gather_list(back_down)

    per_set = 2 * rows * hidden * levels * 2 * sub
    whole3 = lambda i, idx: (0, 0, 0)
    whole2 = lambda i, idx: (0, 0)
    hid_t, grad_pre, out_parts, in_parts, low_down, back_up = pl.pallas_call(
        functools.partial(block_kernel, levels, sub, blocks),
        grid_spec=pltpu.PrefetchScalarGridSpec(
            num_scalar_prefetch=1,
            grid=(blocks,),
            in_specs=[WHOLE] * (2 * levels + 2)
            + [
                pl.BlockSpec((levels, 2 * sub, width), lambda i, idx: (0, 0, i)),
                pl.BlockSpec((levels, width, 2 * sub), lambda i, idx: (0, i, 0)),
                pl.BlockSpec((rank, width), lambda i, idx: (0, i)),
                pl.BlockSpec((width, rank), lambda i, idx: (i, 0)),
            ],
            out_specs=[
                pl.BlockSpec((width, rows), lambda i, idx: (i, 0)),
                pl.BlockSpec((rows, width), lambda i, idx: (0, i)),
                pl.BlockSpec((levels, rows, feat), whole3),
                pl.BlockSpec((levels, rows, feat), whole3),
                pl.BlockSpec((rows, rank), whole2),
                pl.BlockSpec((rows, rank), whole2),
            ],
            scratch_shapes=[
                pltpu.VMEM((levels * 3, rows, sub), F32),
                pltpu.VMEM((levels * 3, rows, sub), F32),
                pltpu.VMEM((rows, rank), F32),
                pltpu.VMEM((rows, rank), F32),
            ],
        ),
        out_shape=(
            sds((hidden, rows), BF16),
            sds((rows, hidden), BF16),
            sds((levels, rows, feat), BF16),
            sds((levels, rows, feat), BF16),
            sds((rows, rank), BF16),
            sds((rows, rank), BF16),
        ),
        compiler_params=params,
        cost_estimate=cost(4 * per_set, 4 * levels * hidden * 2 * sub),
    )(index, *feats, *grads, low_up, back_down, up_tiles, down_tiles, up_right, down_left)

    low_down, back_up = lax.psum((low_down, back_up), "hid")
    grad_pre_items = gather_list(grad_pre)
    hid_items = exchange_list(lambda q: lax.dynamic_slice_in_dim(hid_t, q * own, own, 0))
    out_got = [swap(out_parts[k], "hid", 1 << (k - 1)) for k in range(1, levels)]
    in_got = [swap(in_parts[k], "hid", 1 << (k - 1)) for k in range(1, levels)]

    chunk = math.gcd(own, width)
    grad_down_tiles, grad_down_left = pl.pallas_call(
        functools.partial(down_kernel, levels, sub, groups, blocks, chunk, width),
        grid_spec=pltpu.PrefetchScalarGridSpec(
            num_scalar_prefetch=1,
            grid=(own // chunk,),
            in_specs=[pl.BlockSpec((chunk, rows), lambda i, idx: (i, 0))] * groups
            + [WHOLE] * (2 * groups),
            out_specs=[
                pl.BlockSpec((levels, chunk, 2 * sub), lambda i, idx: (0, i, 0)),
                pl.BlockSpec((chunk, rank), lambda i, idx: (i, 0)),
            ],
        ),
        out_shape=(sds((levels, own, 2 * sub), BF16), sds((own, rank), BF16)),
        compiler_params=params,
        cost_estimate=cost(per_set, 2 * levels * (rows * groups * feat + own * 2 * sub)),
    )(index, *hid_items, *grad_items, *back_down_items)

    grad_up_tiles, grad_up_right = pl.pallas_call(
        functools.partial(up_kernel, levels, groups, blocks),
        grid_spec=pltpu.PrefetchScalarGridSpec(
            num_scalar_prefetch=1,
            grid=(blocks,),
            in_specs=[WHOLE] * groups
            + [pl.BlockSpec((rows, width), lambda i, idx: (0, i))] * groups
            + [WHOLE] * groups,
            out_specs=[
                pl.BlockSpec((levels, part, width), lambda i, idx: (0, 0, i)),
                pl.BlockSpec((own_rank, width), lambda i, idx: (0, i)),
            ],
        ),
        out_shape=(sds((levels, part, hidden), BF16), sds((own_rank, hidden), BF16)),
        compiler_params=params,
        cost_estimate=cost(per_set, 2 * levels * part * hidden + 4 * rows * groups * hidden),
    )(index, *feat_items, *grad_pre_items, *low_up_items)

    low_down_items = exchange_list(
        lambda q: lax.dynamic_slice_in_dim(low_down.T, q * own_rank, own_rank, 0)
    )
    back_up_items = gather_list(back_up)
    grad_down_right = sum(
        dot_nn(low_down_items[d], grad_items[d][0]) for d in range(groups)
    ).astype(BF16)
    grad_up_left = sum(
        dot_nn(own_items[d], back_up_items[d]) for d in range(groups)
    ).astype(BF16)

    def finish(own_part, got, left, right_dot):
        total = own_part.astype(F32)
        for item in got:
            total = total + item.astype(F32)
        return (total + right_dot(left)).astype(BF16)

    layer_out = finish(out_parts[0], out_got, low_down, lambda v: dot_nn(v, down_right))
    grad_tokens = finish(in_parts[0], in_got, back_up, lambda v: dot_nt(v, up_left))
    return (
        layer_out,
        grad_tokens,
        grad_up_tiles,
        grad_down_tiles,
        grad_up_left,
        grad_up_right,
        grad_down_left,
        grad_down_right,
    )


def solution(mesh):
    return jax.shard_map(
        on_device,
        mesh=mesh,
        in_specs=(
            P("tok", "hid"),
            P("tok", "hid"),
            P(None, None, "hid"),
            P(None, "hid", None),
            P(None, "hid", None),
            P("hid", None),
            P(None, "hid"),
            P("hid", None),
            P(None, "hid"),
        ),
        out_specs=(
            P("tok", "hid"),
            P("tok", "hid"),
            P(None, "tok", "hid"),
            P(None, ("hid", "tok"), None),
            P(("hid", "tok"), None),
            P("tok", "hid"),
            P(("hid", "tok"), None),
            P("tok", "hid"),
        ),
        check_vma=False,
    )
```

time: 1080 us -> 498 us (0.46); the launches traced: 1070 us -> 498 us
  matrix products: 480 us -> 19.6 us
  local copies, waits for them, and re-layouts: 352 us -> 23.1 us
  waiting for transfers between devices: 162 us -> 323 us
  Pallas kernels: 0 us -> 78.1 us
  other arithmetic: 42.3 us -> 3.51 us
  starting transfers between devices: 15.1 us -> 35.8 us
    dot_general x52 -> x12, matrix products: 480 us -> 19.6 us  [the longest x10 15.2 us: dot_nn(): return jnp.dot(a, b, preferred_element_type=F32)]
    another operation x20 -> x0, local copies, waits for them, and re-layouts: 206 us -> none  [the longest x4 48.2 us: on_device(): up_tiles[partition_key].reshape(2, sub_width, block_count, block_width)]
    ppermute x12 -> x39, waiting for transfers between devices: 0.03 us -> 158 us  [swap(): return lax.ppermute(block, axis, [(i, i ^ mask) for i in range(count)])]
    psum x2, waiting for transfers between devices: 51.7 us -> 165 us  [the longest x1 106 us: on_device(): lax.psum((dot_nn(tokens, up_left).astype(BF16), dot_nt(cotangent, down_ri...]
    reduce_scatter x5 -> x0, waiting for transfers between devices: 110 us -> none  [the longest x1 110 us: on_device(): lax.psum_scatter(down_terms.astype(jnp.bfloat16), 'tok', scatter_dimensio...]
    pallas_call x0 -> x4, Pallas kernels: none -> 78.1 us  [the longest x1 42.2 us: on_device(): pl.pallas_call(functools.partial(block_kernel, levels, sub, blocks), grid...]
    transpose x4 -> x0, local copies, waits for them, and re-layouts: 50.6 us -> none  [on_device(): jnp.einsum('tbjs,tbh->jsbh', chosen_inputs[partition_key], grad_pre, pref...]
    another operation x2 -> x1, other arithmetic: 41.7 us -> 2.96 us  [on_device(): grad_items = gather_list(jnp.stack(grads))]
  transfers between devices with their start and end apart: 20 -> 41, of which waited for: 2 -> 13; matrix products, arithmetic and copies ran while one was open for 54% -> 8% of each run, Pallas kernels for 0% -> 13%
where the time goes in v1:
time: 498 us
  waiting for transfers between devices  323 us (65%)
  Pallas kernels  78.1 us (16%)
  starting transfers between devices  35.8 us (7%)
  local copies, waits for them, and re-layouts  23.1 us (5%)
  matrix products  19.6 us (4%)
  between operations  14.5 us (3%)
    ppermute x39, waiting for transfers between devices, swap(): return lax.ppermute(block, axis, [(i, i ^ mask) for i in range(count)])  158 us
    psum x1, waiting for transfers between devices, on_device(): lax.psum((dot_nn(tokens, up_left).astype(BF16), dot_nt(cotangent, down_ri...  106 us
    psum x1, waiting for transfers between devices, on_device(): low_down, back_up = lax.psum((low_down, back_up), 'hid')  58.5 us
    pallas_call x1, Pallas kernels, on_device(): pl.pallas_call(functools.partial(block_kernel, levels, sub, blocks), grid...  42.2 us
    ppermute x39, starting transfers between devices, swap(): return lax.ppermute(block, axis, [(i, i ^ mask) for i in range(count)])  35.7 us
    pallas_call x1, Pallas kernels, on_device(): pl.pallas_call(functools.partial(up_kernel, levels, groups, blocks), grid...  16.9 us
    dot_general x10, matrix products, dot_nn(): return jnp.dot(a, b, preferred_element_type=F32)  15.2 us
    pallas_call x1, Pallas kernels, on_device(): pl.pallas_call(functools.partial(down_kernel, levels, sub, groups, blocks...  14.6 us
  transfers between devices with their start and end apart: 41, of which 13 were waited for; matrix products, arithmetic and copies ran while one was open for 8% of the time, Pallas kernels for 13%

profile of v1, /device:TPU:0, one launch (start us, length us, event | category | flops | bytes accessed | tf_op | source)
XLA Modules:
  0.0 497.6 jit_solution(4177605926443680123)
XLA Ops:
  7.3 3.0 collective-permute-start.3
  10.3 2.0 collective-permute-start.1
  12.4 3.0 collective-permute-start.5
  15.4 2.5 convolution_convert_fusion.1
  17.9 11.0 %collective-permute-done.3.refs_5_ = bf16[256,1536]{1,0:T(8,128)(2,1)S(1)} collective-permute-done((bf16[256,1536]{1,0:T(8,128)(2,1)}, bf16[256,1536]{1,0:T(8,128)(2,1)S(1)}, u32[]{:S(2)}, u32[]{:S(2)}) %collective-permute-start.3) | collective-permute-done | bytes 786464 | tf_op jit(solution)/shard_map/ppermute | solution.py:21
  28.9 3.2 collective-permute-start.2
  34.0 106.3 %all-reduce.7.cloned.1.call-done = (bf16[256,256]{0,1:T(8,128)(2,1)}, bf16[256,256]{1,0:T(8,128)(2,1)}) async-done(((bf16[256,256]{0,1:T(8,128)(2,1)}, bf16[256,256]{1,0:T(8,128)(2,1)}), (bf16[256,256]{0,1:T(8,128)(2,1)}, bf16[256,256]{1,0:T(8,128)(2,1)})) %all-reduce.7.cloned.1.call-update) | async-done | bytes 262160 | tf_op jit(solution)/shard_map/psum | solution.py:175
  140.3 1.7 copy.22.refs_8_
  144.9 3.0 pad_maximum_fusion.refs_4_
  149.8 4.3 shard_map.153
  155.9 42.2 %shard_map.152 = (bf16[3072,256]{1,0:T(8,128)(2,1)}, bf16[256,3072]{1,0:T(8,128)(2,1)}, bf16[4,256,1536]{2,1,0:T(8,128)(2,1)}, bf16[4,256,1536]{2,1,0:T(8,128)(2...) custom-call(s32[97]{0:T(128)} %pad_add_fusion.index, bf16[256,1536]{1,0:T(8,128)(2,1)} %refs_0_.3, ...), custom_call_target="tpu_custom_call" | custom-call | flops 25769803776 | bytes 50331648 | tf_op jit(solution)/shard_map/pallas_call | solution.py:205
  200.5 2.9 slice_bitcast_fusion.11
  203.9 19.8 %collective-permute-done.32 = bf16[384,256]{1,0:T(8,128)(2,1)S(1)} collective-permute-done((bf16[384,256]{1,0:T(8,128)(2,1)S(1)}, bf16[384,256]{1,0:T(8,128)(2,1)S(1)}, u32[]{:S(2)}, u32[]{:S(2)}) %collective-permute-start.32) | collective-permute-done | bytes 196640 | tf_op jit(solution)/shard_map/ppermute | solution.py:21
  223.6 1.8 collective-permute-start.8
  225.4 58.5 %all-reduce.5.cloned.1.call-done = (bf16[256,256]{1,0:T(8,128)(2,1)}, bf16[256,256]{1,0:T(8,128)(2,1)}) async-done(((bf16[256,256]{1,0:T(8,128)(2,1)}, bf16[256,256]{1,0:T(8,128)(2,1)}), (bf16[256,256]{1,0:T(8,128)(2,1)}, bf16[256,256]{1,0:T(8,128)(2,1)})) %all-reduce.5.cloned.1.call-update) | async-done | bytes 262160 | tf_op jit(solution)/shard_map/psum | solution.py:244
  284.0 1.7 dynamic-slice_bitcast_fusion.5
  287.4 4.4 collective-permute-done.33
  292.9 3.1 slice_bitcast_fusion.8
  298.9 22.9 %collective-permute-done.7 = bf16[256,1536]{1,0:T(8,128)(2,1)S(1)} collective-permute-done((bf16[256,1536]{1,0:T(8,128)(2,1)S(1)}, bf16[256,1536]{1,0:T(8,128)(2,1)S(1)}, u32[]{:S(2)}, u32[]{:S(2)}) %collective-permute-start.7) | collective-permute-done | bytes 786464 | tf_op jit(solution)/shard_map/ppermute | solution.py:21
  322.6 5.7 %dynamic-slice_bitcast_fusion = (bf16[12,256,256]{2,1,0:T(8,128)(2,1)}, bf16[12,256,256]{2,1,0:T(8,128)(2,1)}, bf16[12,256,256]{2,1,0:T(8,128)(2,1)}, bf16[12,256,256]{2,1,0:T(8,128)(2,1)}) fusion(bf16[2,12,256,256]{3,2,1,0:T(8,128)(2,1)} %get-tuple-element.24, s32[]{:T(128)S(6)} %select_n.79, s32[]{:T(128)S(6)} %select_n.77, s32[]{:T(128)S(6)} %select_n.75, ...), kind=kLoop, calls=%fused_computation.15 | loop fusion | bytes 12582928 | tf_op jit(solution)/shard_map/jit(dynamic_index_in_dim)/squeeze | solution.py:191
  328.3 7.1 %collective-permute-done.11 = bf16[256,1536]{1,0:T(8,128)(2,1)} collective-permute-done((bf16[256,1536]{1,0:T(8,128)(2,1)}, bf16[256,1536]{1,0:T(8,128)(2,1)}, u32[]{:S(2)}, u32[]{:S(2)}) %collective-permute-start.11) | collective-permute-done | bytes 786464 | tf_op jit(solution)/shard_map/ppermute | solution.py:21
  337.0 9.5 %collective-permute-done.10 = bf16[256,1536]{1,0:T(8,128)(2,1)} collective-permute-done((bf16[256,1536]{1,0:T(8,128)(2,1)}, bf16[256,1536]{1,0:T(8,128)(2,1)}, u32[]{:S(2)}, u32[]{:S(2)}) %collective-permute-start.10) | collective-permute-done | bytes 786464 | tf_op jit(solution)/shard_map/ppermute | solution.py:21
  349.8 14.4 %collective-permute-done.9 = bf16[256,1536]{1,0:T(8,128)(2,1)} collective-permute-done((bf16[256,1536]{1,0:T(8,128)(2,1)}, bf16[256,1536]{1,0:T(8,128)(2,1)}, u32[]{:S(2)}, u32[]{:S(2)}) %collective-permute-start.9) | collective-permute-done | bytes 786464 | tf_op jit(solution)/shard_map/ppermute | solution.py:21
  365.7 7.4 %collective-permute-done.16.refs_6_ = bf16[256,3072]{1,0:T(8,128)(2,1)} collective-permute-done((bf16[256,3072]{1,0:T(8,128)(2,1)}, bf16[256,3072]{1,0:T(8,128)(2,1)}, u32[]{:S(2)}, u32[]{:S(2)}) %collective-permute-start.16) | collective-permute-done | bytes 1572896 | tf_op jit(solution)/shard_map/ppermute | solution.py:21
  377.9 2.9 fusion.9
  380.8 3.3 fusion.5
  385.6 21.1 %collective-permute-done.13.refs_2_ = bf16[12,256,256]{2,1,0:T(8,128)(2,1)S(1)} collective-permute-done((bf16[12,256,256]{2,1,0:T(8,128)(2,1)S(1)}, bf16[12,256,256]{2,1,0:T(8,128)(2,1)S(1)}, u32[]{:S(2)}, u32[]{:S(2)}) %collective-permute-start.13) | collective-permute-done | bytes 1572896 | tf_op jit(solution)/shard_map/ppermute | solution.py:21
  408.2 30.9 %collective-permute-done.14.refs_3_ = bf16[12,256,256]{2,1,0:T(8,128)(2,1)S(1)} collective-permute-done((bf16[12,256,256]{2,1,0:T(8,128)(2,1)S(1)}, bf16[12,256,256]{2,1,0:T(8,128)(2,1)S(1)}, u32[]{:S(2)}, u32[]{:S(2)}) %collective-permute-start.14) | collective-permute-done | bytes 1572896 | tf_op jit(solution)/shard_map/ppermute | solution.py:21
  442.6 16.9 %shard_map.154 = (bf16[4,256,3072]{2,1,0:T(8,128)(2,1)}, bf16[64,3072]{1,0:T(8,128)(2,1)}) custom-call(s32[97]{0:T(128)} %pad_add_fusion.index, bf16[12,256,256]{2,1,0:T(8,128)(2,1)} %get-tuple-element.39.refs_0_, bf16[12,256,256]{2,1,0:T(8,128)(2,1)} %collective-permute-done.12.refs_1_, bf16[12,256,256]{2,1,0:T(8,128)(2,1)} %copy-done.24, ...), custom_call_target="tpu_custom_call" | custom-call | flops 6442450944 | bytes 18874368 | tf_op jit(solution)/shard_map/pallas_call | solution.py:268
  463.4 9.4 %collective-permute-done.37 = bf16[64,256]{0,1:T(8,128)(2,1)S(1)} collective-permute-done((bf16[64,256]{0,1:T(8,128)(2,1)S(1)}, bf16[64,256]{0,1:T(8,128)(2,1)S(1)}, u32[]{:S(2)}, u32[]{:S(2)}) %collective-permute-start.37) | collective-permute-done | bytes 32800 | tf_op jit(solution)/shard_map/ppermute | solution.py:21
  472.9 2.1 fusion.1
  476.1 14.6 %shard_map.155 = (bf16[4,768,1024]{2,1,0:T(8,128)(2,1)}, bf16[768,256]{1,0:T(8,128)(2,1)}) custom-call(s32[97]{0:T(128)} %pad_add_fusion.index, bf16[768,256]{1,0:T(8,128)(2,1)} %get-tuple-element.49.refs_0_, bf16[768,256]{1,0:T(8,128)(2,1)} %copy-done.27, bf16[768,256]{1,0:T(8,128)(2,1)} %copy-done.28, bf16[768,256]{1,0:T(8,128)(2,1)} %copy-done.29, ...), custom_call_target="tpu_custom_call" | custom-call | flops 6442450944 | bytes 18874368 | tf_op jit(solution)/shard_map/pallas_call | solution.py:251
  (154 shorter events, 40.4 us)
Async XLA Ops:
  7.2 133.1 %all-reduce.7.cloned.1.call-start = ((), (), s32[]{:S(2)}) async-start(), calls=%async_computation.1 | async-start | bytes 524288 | tf_op jit(solution)/shard_map/psum | solution.py:175
  7.3 21.6 %collective-permute-start.3 = (bf16[256,1536]{1,0:T(8,128)(2,1)}, bf16[256,1536]{1,0:T(8,128)(2,1)S(1)}, u32[]{:S(2)}, u32[]{:S(2)}) collective-permute-start(bf16[256,1536]{1,0:T(8,128)(2,1)} %refs_4_.1), channel_id=1, source_target_pairs={{0,4},{4,0},{8,12},{12,8},{16,20},{20,16},{24,28},{28,24},{1,5},{5... | collective-permute-start | bytes 2359304 | tf_op jit(solution)/shard_map/ppermute | solution.py:21
  10.3 137.6 %collective-permute-start = (bf16[256,1536]{1,0:T(8,128)(2,1)}, bf16[256,1536]{1,0:T(8,128)(2,1)}, u32[]{:S(2)}, u32[]{:S(2)}) collective-permute-start(bf16[256,1536]{1,0:T(8,128)(2,1)} %refs_0_.3), channel_id=1, source_target_pairs={{0,4},{4,0},{8,12},{12,8},{16,20},{20,16},{24,28},{28,24},{1,5},{5... | collective-permute-start | bytes 2359304 | tf_op jit(solution)/shard_map/ppermute | solution.py:21
  10.3 138.0 %collective-permute-start.1 = (bf16[256,1536]{1,0:T(8,128)(2,1)}, bf16[256,1536]{1,0:T(8,128)(2,1)}, u32[]{:S(2)}, u32[]{:S(2)}) collective-permute-start(bf16[256,1536]{1,0:T(8,128)(2,1)} %refs_0_.3), channel_id=1, source_target_pairs={{0,8},{4,12},{8,0},{12,4},{16,24},{20,28},{24,16},{28,20},{1,9},{5... | collective-permute-start | bytes 2359304 | tf_op jit(solution)/shard_map/ppermute | solution.py:21
  12.4 131.0 %collective-permute-start.4 = (bf16[256,1536]{1,0:T(8,128)(2,1)}, bf16[256,1536]{1,0:T(8,128)(2,1)}, u32[]{:S(2)}, u32[]{:S(2)}) collective-permute-start(bf16[256,1536]{1,0:T(8,128)(2,1)} %refs_4_.1), channel_id=1, source_target_pairs={{0,8},{4,12},{8,0},{12,4},{16,24},{20,28},{24,16},{28,20},{1,9},{5... | collective-permute-start | bytes 2359304 | tf_op jit(solution)/shard_map/ppermute | solution.py:21
  12.4 131.0 %collective-permute-start.5 = (bf16[256,1536]{1,0:T(8,128)(2,1)}, bf16[256,1536]{1,0:T(8,128)(2,1)}, u32[]{:S(2)}, u32[]{:S(2)}) collective-permute-start(bf16[256,1536]{1,0:T(8,128)(2,1)} %refs_4_.1), channel_id=1, source_target_pairs={{0,16},{4,20},{8,24},{12,28},{16,0},{20,4},{24,8},{28,12},{1,17},{... | collective-permute-start | bytes 2359304 | tf_op jit(solution)/shard_map/ppermute | solution.py:21
  28.9 120.9 %collective-permute-start.2 = (bf16[256,1536]{1,0:T(8,128)(2,1)S(1)}, bf16[256,1536]{1,0:T(8,128)(2,1)}, u32[]{:S(2)}, u32[]{:S(2)}) collective-permute-start(bf16[256,1536]{1,0:T(8,128)(2,1)S(1)} %copy-done.4), channel_id=1, source_target_pairs={{0,16},{4,20},{8,24},{12,28},{16,0},{20,4},{24,8},{28,12},{1,17},{... | collective-permute-start | bytes 2359304 | tf_op jit(solution)/shard_map/ppermute | solution.py:21
  33.1 250.9 %all-reduce.5.cloned.1.call-start = ((), (), s32[]{:S(2)}) async-start(), calls=%async_computation | async-start | bytes 524288 | tf_op jit(solution)/shard_map/psum | solution.py:244
  143.4 54.8 %collective-permute-start.18 = (bf16[64,256]{1,0:T(8,128)(2,1)S(1)}, bf16[64,256]{1,0:T(8,128)(2,1)S(1)}, u32[]{:S(2)}, u32[]{:S(2)}) collective-permute-start(bf16[64,256]{1,0:T(8,128)(2,1)S(1)} %get-tuple-element.58), channel_id=1, source_target_pairs={{0,1},{1,0},{2,3},{3,2},{4,5},{5,4},{6,7},{7,6},{8,9},{9,8},{10,11... | collective-permute-start | bytes 98312 | tf_op jit(solution)/shard_map/ppermute | solution.py:21
  143.4 54.8 %collective-permute-start.19 = (bf16[64,256]{1,0:T(8,128)(2,1)S(1)}, bf16[64,256]{1,0:T(8,128)(2,1)S(1)}, u32[]{:S(2)}, u32[]{:S(2)}) collective-permute-start(bf16[64,256]{1,0:T(8,128)(2,1)S(1)} %get-tuple-element.57), channel_id=1, source_target_pairs={{0,2},{1,3},{2,0},{3,1},{4,6},{5,7},{6,4},{7,5},{8,10},{9,11},{10,... | collective-permute-start | bytes 98312 | tf_op jit(solution)/shard_map/ppermute | solution.py:21
  147.9 55.4 %collective-permute-start.20 = (bf16[64,256]{1,0:T(8,128)(2,1)S(1)}, bf16[64,256]{1,0:T(8,128)(2,1)S(1)}, u32[]{:S(2)}, u32[]{:S(2)}) collective-permute-start(bf16[64,256]{1,0:T(8,128)(2,1)S(1)} %get-tuple-element.56), channel_id=1, source_target_pairs={{0,3},{1,2},{2,1},{3,0},{4,7},{5,6},{6,5},{7,4},{8,11},{9,10},{10,... | collective-permute-start | bytes 98312 | tf_op jit(solution)/shard_map/ppermute | solution.py:21
  148.3 199.0 %collective-permute-start.25 = (bf16[4,256,1536]{2,1,0:T(8,128)(2,1)}, bf16[4,256,1536]{2,1,0:T(8,128)(2,1)}, u32[]{:S(2)}, u32[]{:S(2)}) collective-permute-start(bf16[4,256,1536]{2,1,0:T(8,128)(2,1)} %pad_maximum_fusion.refs_4_), channel_id=1, source_target_pairs={{0,2},{1,3},{2,0},{3,1},{4,6},{5,7},{6,4},{7,5},{8,10},{9,11},{10,... | collective-permute-start | bytes 9437192 | tf_op jit(solution)/shard_map/ppermute | solution.py:21
  155.3 68.4 %collective-permute-start.32 = (bf16[384,256]{1,0:T(8,128)(2,1)S(1)}, bf16[384,256]{1,0:T(8,128)(2,1)S(1)}, u32[]{:S(2)}, u32[]{:S(2)}) collective-permute-start(bf16[384,256]{1,0:T(8,128)(2,1)S(1)} %get-tuple-element.51), channel_id=1, source_target_pairs={{0,2},{1,3},{2,0},{3,1},{4,6},{5,7},{6,4},{7,5},{8,10},{9,11},{10,... | collective-permute-start | bytes 589832 | tf_op jit(solution)/shard_map/ppermute | solution.py:21
  198.2 87.5 %collective-permute-start.30 = (bf16[384,256]{1,0:T(8,128)(2,1)S(1)}, bf16[384,256]{1,0:T(8,128)(2,1)S(1)}, u32[]{:S(2)}, u32[]{:S(2)}) collective-permute-start(bf16[384,256]{1,0:T(8,128)(2,1)S(1)} %get-tuple-element.52), channel_id=1, source_target_pairs={{0,1},{1,0},{2,3},{3,2},{4,5},{5,4},{6,7},{7,6},{8,9},{9,8},{10,11... | collective-permute-start | bytes 589832 | tf_op jit(solution)/shard_map/ppermute | solution.py:21
  199.4 86.3 %collective-permute-start.34 = (bf16[384,256]{1,0:T(8,128)(2,1)S(1)}, bf16[384,256]{1,0:T(8,128)(2,1)S(1)}, u32[]{:S(2)}, u32[]{:S(2)}) collective-permute-start(bf16[384,256]{1,0:T(8,128)(2,1)S(1)} %get-tuple-element.50), channel_id=1, source_target_pairs={{0,3},{1,2},{2,1},{3,0},{4,7},{5,6},{6,5},{7,4},{8,11},{9,10},{10,... | collective-permute-start | bytes 589832 | tf_op jit(solution)/shard_map/ppermute | solution.py:21
  203.4 169.8 %collective-permute-start.24 = (bf16[4,256,1536]{2,1,0:T(8,128)(2,1)}, bf16[4,256,1536]{2,1,0:T(8,128)(2,1)}, u32[]{:S(2)}, u32[]{:S(2)}) collective-permute-start(bf16[4,256,1536]{2,1,0:T(8,128)(2,1)} %pad_maximum_fusion.refs_4_), channel_id=1, source_target_pairs={{0,1},{1,0},{2,3},{3,2},{4,5},{5,4},{6,7},{7,6},{8,9},{9,8},{10,11... | collective-permute-start | bytes 9437192 | tf_op jit(solution)/shard_map/ppermute | solution.py:21
  223.6 73.9 %collective-permute-start.8 = (bf16[256,1536]{1,0:T(8,128)(2,1)}, bf16[256,1536]{1,0:T(8,128)(2,1)S(1)}, u32[]{:S(2)}, u32[]{:S(2)}) collective-permute-start(bf16[256,1536]{1,0:T(8,128)(2,1)} %get-tuple-element.44), channel_id=1, source_target_pairs={{0,16},{4,20},{8,24},{12,28},{16,0},{20,4},{24,8},{28,12},{1,17},{... | collective-permute-start | bytes 2359304 | tf_op jit(solution)/shard_map/ppermute | solution.py:21
  291.8 29.9 %collective-permute-start.7 = (bf16[256,1536]{1,0:T(8,128)(2,1)S(1)}, bf16[256,1536]{1,0:T(8,128)(2,1)S(1)}, u32[]{:S(2)}, u32[]{:S(2)}) collective-permute-start(bf16[256,1536]{1,0:T(8,128)(2,1)S(1)} %get-tuple-element.45), channel_id=1, source_target_pairs={{0,8},{4,12},{8,0},{12,4},{16,24},{20,28},{24,16},{28,20},{1,9},{5... | collective-permute-start | bytes 2359304 | tf_op jit(solution)/shard_map/ppermute | solution.py:21
  296.0 32.3 %collective-permute-start.6 = (bf16[256,1536]{1,0:T(8,128)(2,1)}, bf16[256,1536]{1,0:T(8,128)(2,1)}, u32[]{:S(2)}, u32[]{:S(2)}) collective-permute-start(bf16[256,1536]{1,0:T(8,128)(2,1)} %get-tuple-element.43), channel_id=1, source_target_pairs={{0,4},{4,0},{8,12},{12,8},{16,20},{20,16},{24,28},{28,24},{1,5},{5... | collective-permute-start | bytes 2359304 | tf_op jit(solution)/shard_map/ppermute | solution.py:21
  297.6 37.9 %collective-permute-start.11 = (bf16[256,1536]{1,0:T(8,128)(2,1)}, bf16[256,1536]{1,0:T(8,128)(2,1)}, u32[]{:S(2)}, u32[]{:S(2)}) collective-permute-start(bf16[256,1536]{1,0:T(8,128)(2,1)} %get-tuple-element.41), channel_id=1, source_target_pairs={{0,16},{4,20},{8,24},{12,28},{16,0},{20,4},{24,8},{28,12},{1,17},{... | collective-permute-start | bytes 2359304 | tf_op jit(solution)/shard_map/ppermute | solution.py:21
  321.7 24.7 %collective-permute-start.10 = (bf16[256,1536]{1,0:T(8,128)(2,1)}, bf16[256,1536]{1,0:T(8,128)(2,1)}, u32[]{:S(2)}, u32[]{:S(2)}) collective-permute-start(bf16[256,1536]{1,0:T(8,128)(2,1)} %get-tuple-element.42), channel_id=1, source_target_pairs={{0,8},{4,12},{8,0},{12,4},{16,24},{20,28},{24,16},{28,20},{1,9},{5... | collective-permute-start | bytes 2359304 | tf_op jit(solution)/shard_map/ppermute | solution.py:21
  328.3 35.9 %collective-permute-start.12 = (bf16[12,256,256]{2,1,0:T(8,128)(2,1)}, bf16[12,256,256]{2,1,0:T(8,128)(2,1)}, u32[]{:S(2)}, u32[]{:S(2)}) collective-permute-start(bf16[12,256,256]{2,1,0:T(8,128)(2,1)} %get-tuple-element.38), channel_id=1, source_target_pairs={{0,1},{1,0},{2,3},{3,2},{4,5},{5,4},{6,7},{7,6},{8,9},{9,8},{10,11... | collective-permute-start | bytes 4718600 | tf_op jit(solution)/shard_map/ppermute | solution.py:21
  335.5 37.6 %collective-permute-start.16 = (bf16[256,3072]{1,0:T(8,128)(2,1)}, bf16[256,3072]{1,0:T(8,128)(2,1)}, u32[]{:S(2)}, u32[]{:S(2)}) collective-permute-start(bf16[256,3072]{1,0:T(8,128)(2,1)} %get-tuple-element.25.refs_4_), channel_id=1, source_target_pairs={{0,2},{1,3},{2,0},{3,1},{4,6},{5,7},{6,4},{7,5},{8,10},{9,11},{10,... | collective-permute-start | bytes 4718600 | tf_op jit(solution)/shard_map/ppermute | solution.py:21
  347.3 113.5 %collective-permute-start.26 = (bf16[4,256,1536]{2,1,0:T(8,128)(2,1)}, bf16[4,256,1536]{2,1,0:T(8,128)(2,1)}, u32[]{:S(2)}, u32[]{:S(2)}) collective-permute-start(bf16[4,256,1536]{2,1,0:T(8,128)(2,1)} %collective-permute-done.25.refs_6_), channel_id=1, source_target_pairs={{0,1},{1,0},{2,3},{3,2},{4,5},{5,4},{6,7},{7,6},{8,9},{9,8},{10,11... | collective-permute-start | bytes 9437192 | tf_op jit(solution)/shard_map/ppermute | solution.py:21
  364.2 75.8 %collective-permute-start.15 = (bf16[256,3072]{1,0:T(8,128)(2,1)}, bf16[256,3072]{1,0:T(8,128)(2,1)S(1)}, u32[]{:S(2)}, u32[]{:S(2)}) collective-permute-start(bf16[256,3072]{1,0:T(8,128)(2,1)} %get-tuple-element.25.refs_4_), channel_id=1, source_target_pairs={{0,1},{1,0},{2,3},{3,2},{4,5},{5,4},{6,7},{7,6},{8,9},{9,8},{10,11... | collective-permute-start | bytes 4718600 | tf_op jit(solution)/shard_map/ppermute | solution.py:21
  364.2 42.5 %collective-permute-start.13 = (bf16[12,256,256]{2,1,0:T(8,128)(2,1)S(1)}, bf16[12,256,256]{2,1,0:T(8,128)(2,1)S(1)}, u32[]{:S(2)}, u32[]{:S(2)}) collective-permute-start(bf16[12,256,256]{2,1,0:T(8,128)(2,1)S(1)} %copy-done.7), channel_id=1, source_target_pairs={{0,2},{1,3},{2,0},{3,1},{4,6},{5,7},{6,4},{7,5},{8,10},{9,11},{10,... | collective-permute-start | bytes 4718600 | tf_op jit(solution)/shard_map/ppermute | solution.py:21
  373.1 66.0 %collective-permute-start.14 = (bf16[12,256,256]{2,1,0:T(8,128)(2,1)S(1)}, bf16[12,256,256]{2,1,0:T(8,128)(2,1)S(1)}, u32[]{:S(2)}, u32[]{:S(2)}) collective-permute-start(bf16[12,256,256]{2,1,0:T(8,128)(2,1)S(1)} %copy-done.6), channel_id=1, source_target_pairs={{0,3},{1,2},{2,1},{3,0},{4,7},{5,6},{6,5},{7,4},{8,11},{9,10},{10,... | collective-permute-start | bytes 4718600 | tf_op jit(solution)/shard_map/ppermute | solution.py:21
  373.2 68.3 %collective-permute-start.17 = (bf16[256,3072]{1,0:T(8,128)(2,1)}, bf16[256,3072]{1,0:T(8,128)(2,1)S(1)}, u32[]{:S(2)}, u32[]{:S(2)}) collective-permute-start(bf16[256,3072]{1,0:T(8,128)(2,1)} %collective-permute-done.16.refs_6_), channel_id=1, source_target_pairs={{0,1},{1,0},{2,3},{3,2},{4,5},{5,4},{6,7},{7,6},{8,9},{9,8},{10,11... | collective-permute-start | bytes 4718600 | tf_op jit(solution)/shard_map/ppermute | solution.py:21
  406.7 56.1 %collective-permute-start.28 = (bf16[256,256]{1,0:T(8,128)(2,1)S(1)}, bf16[256,256]{1,0:T(8,128)(2,1)S(1)}, u32[]{:S(2)}, u32[]{:S(2)}) collective-permute-start(bf16[256,256]{1,0:T(8,128)(2,1)S(1)} %copy-done.30), channel_id=1, source_target_pairs={{0,2},{1,3},{2,0},{3,1},{4,6},{5,7},{6,4},{7,5},{8,10},{9,11},{10,... | collective-permute-start | bytes 393224 | tf_op jit(solution)/shard_map/ppermute | solution.py:21
  439.2 35.9 %collective-permute-start.21 = (bf16[768,256]{1,0:T(8,128)(2,1)}, bf16[768,256]{1,0:T(8,128)(2,1)S(1)}, u32[]{:S(2)}, u32[]{:S(2)}) collective-permute-start(bf16[768,256]{1,0:T(8,128)(2,1)} %get-tuple-element.48), channel_id=1, source_target_pairs={{0,1},{1,0},{2,3},{3,2},{4,5},{5,4},{6,7},{7,6},{8,9},{9,8},{10,11... | collective-permute-start | bytes 1179656 | tf_op jit(solution)/shard_map/ppermute | solution.py:21
  440.0 35.1 %collective-permute-start.22 = (bf16[768,256]{1,0:T(8,128)(2,1)}, bf16[768,256]{1,0:T(8,128)(2,1)S(1)}, u32[]{:S(2)}, u32[]{:S(2)}) collective-permute-start(bf16[768,256]{1,0:T(8,128)(2,1)} %get-tuple-element.47), channel_id=1, source_target_pairs={{0,2},{1,3},{2,0},{3,1},{4,6},{5,7},{6,4},{7,5},{8,10},{9,11},{10,... | collective-permute-start | bytes 1179656 | tf_op jit(solution)/shard_map/ppermute | solution.py:21
  441.5 18.5 %collective-permute-start.38 = (bf16[64,256]{0,1:T(8,128)(2,1)S(1)}, bf16[64,256]{0,1:T(8,128)(2,1)S(1)}, u32[]{:S(2)}, u32[]{:S(2)}) collective-permute-start(bf16[64,256]{0,1:T(8,128)(2,1)S(1)} %copy-done.21), channel_id=1, source_target_pairs={{0,3},{1,2},{2,1},{3,0},{4,7},{5,6},{6,5},{7,4},{8,11},{9,10},{10,... | collective-permute-start | bytes 98312 | tf_op jit(solution)/shard_map/ppermute | solution.py:21
  (46 other events, 662.3 us)
Sparse Core Ops, SparseCore 0:
  33.2 107.0 all-reduce.6
  198.3 85.6 all-reduce.4

commit v2 on v1

--- a/solution.py
+++ b/solution.py
@@ -37,6 +37,14 @@
     return [pick(me)] + [
         swap(pick(me ^ d), "tok", d) for d in range(1, lax.axis_size("tok"))
     ]
+
+
+def sum_hid(block):
+    mask = 1
+    while mask < lax.axis_size("hid"):
+        block = (block.astype(F32) + swap(block, "hid", mask).astype(F32)).astype(BF16)
+        mask *= 2
+    return block
 
 
 def gelu_parts(pre_act):
@@ -172,8 +180,10 @@
     )
     sds = jax.ShapeDtypeStruct
 
-    lows = lax.psum(
-        (dot_nn(tokens, up_left).astype(BF16), dot_nt(cotangent, down_right).astype(BF16)), "hid"
+    lows = sum_hid(
+        jnp.stack(
+            [dot_nn(tokens, up_left).astype(BF16), dot_nt(cotangent, down_right).astype(BF16)]
+        )
     )
     low_up, back_down = lows
     feats = [tokens] + [swap(tokens, "hid", 1 << k) for k in range(levels - 1)]
@@ -241,7 +251,7 @@
         cost_estimate=cost(4 * per_set, 4 * levels * hidden * 2 * sub),
     )(index, *feats, *grads, low_up, back_down, up_tiles, down_tiles, up_right, down_left)
 
-    low_down, back_up = lax.psum((low_down, back_up), "hid")
+    low_down, back_up = sum_hid(jnp.stack([low_down, back_up]))
     grad_pre_items = gather_list(grad_pre)
     hid_items = exchange_list(lambda q: lax.dynamic_slice_in_dim(hid_t, q * own, own, 0))
     out_got = [swap(out_parts[k], "hid", 1 << (k - 1)) for k in range(1, levels)]

time: 498 us -> 454 us (0.912)
  waiting for transfers between devices: 323 us -> 292 us
  between operations: 14.5 us -> 1.31 us
    psum x2 -> x0, waiting for transfers between devices: 165 us -> none  [the longest x1 106 us: on_device(): lax.psum((dot_nn(tokens, up_left).astype(BF16), dot_nt(cotangent, down_ri...]
    ppermute x39 -> x45, waiting for transfers between devices: 158 us -> 292 us  [swap(): return lax.ppermute(block, axis, [(i, i ^ mask) for i in range(count)])]
    ppermute x39 -> x45, starting transfers between devices: 35.7 us -> 39.6 us  [swap(): return lax.ppermute(block, axis, [(i, i ^ mask) for i in range(count)])]
  transfers between devices with their start and end apart: 41 -> 45, of which waited for: 13 -> 19; matrix products, arithmetic and copies ran while one was open for 8% -> 8% of each run, Pallas kernels for 13% -> 14%
where the time goes in v2:
time: 454 us; the launch traced here: 453 us
  waiting for transfers between devices  292 us (64%)
  Pallas kernels  79.3 us (17%)
  starting transfers between devices  39.6 us (9%)
  local copies, waits for them, and re-layouts  18.6 us (4%)
  matrix products  15.9 us (4%)
  other arithmetic  6.19 us (1%)
    ppermute x45, waiting for transfers between devices, swap(): return lax.ppermute(block, axis, [(i, i ^ mask) for i in range(count)])  292 us
    pallas_call x1, Pallas kernels, on_device(): pl.pallas_call(functools.partial(block_kernel, levels, sub, blocks), grid...  43.3 us
    ppermute x45, starting transfers between devices, swap(): return lax.ppermute(block, axis, [(i, i ^ mask) for i in range(count)])  39.6 us
    pallas_call x1, Pallas kernels, on_device(): pl.pallas_call(functools.partial(up_kernel, levels, groups, blocks), grid...  16.8 us
    pallas_call x1, Pallas kernels, on_device(): pl.pallas_call(functools.partial(down_kernel, levels, sub, groups, blocks...  14.6 us
    dot_general x10, matrix products, dot_nn(): return jnp.dot(a, b, preferred_element_type=F32)  11 us
  transfers between devices with their start and end apart: 45, of which 19 were waited for; matrix products, arithmetic and copies ran while one was open for 8% of the time, Pallas kernels for 14%

profile of v2, /device:TPU:0, one launch (start us, length us, event | category | flops | bytes accessed | tf_op | source)
XLA Modules:
  0.0 453.1 jit_solution(1545767151077237075)
XLA Ops:
  3.8 3.0 collective-permute-start.6
  6.8 7.1 %collective-permute-done.6 = bf16[2,256,256]{2,1,0:T(8,128)(2,1)S(1)} collective-permute-done((bf16[2,256,256]{2,1,0:T(8,128)(2,1)S(1)}, bf16[2,256,256]{2,1,0:T(8,128)(2,1)S(1)}, u32[]{:S(2)}, u32[]{:S(2)}) %collective-permute-start.6) | collective-permute-done | bytes 262176 | tf_op jit(solution)/shard_map/ppermute | solution.py:21
  14.0 2.2 collective-permute-start.7
  16.2 4.5 collective-permute-done.7
  20.8 3.3 collective-permute-start.8
  27.2 7.3 %collective-permute-done.8 = bf16[2,256,256]{2,1,0:T(8,128)(2,1)S(1)} collective-permute-done((bf16[2,256,256]{2,1,0:T(8,128)(2,1)S(1)}, bf16[2,256,256]{2,1,0:T(8,128)(2,1)S(1)}, u32[]{:S(2)}, u32[]{:S(2)}) %collective-permute-start.8) | collective-permute-done | bytes 262176 | tf_op jit(solution)/shard_map/ppermute | solution.py:21
  35.0 3.4 collective-permute-start.5
  41.5 20.1 %collective-permute-done.1.refs_2_ = bf16[256,1536]{1,0:T(8,128)(2,1)} collective-permute-done((bf16[256,1536]{1,0:T(8,128)(2,1)S(1)}, bf16[256,1536]{1,0:T(8,128)(2,1)}, u32[]{:S(2)}, u32[]{:S(2)}) %collective-permute-start.1) | collective-permute-done | bytes 786464 | tf_op jit(solution)/shard_map/ppermute | solution.py:21
  61.6 6.7 %collective-permute-done.2.refs_3_ = bf16[256,1536]{1,0:T(8,128)(2,1)} collective-permute-done((bf16[256,1536]{1,0:T(8,128)(2,1)S(1)}, bf16[256,1536]{1,0:T(8,128)(2,1)}, u32[]{:S(2)}, u32[]{:S(2)}) %collective-permute-start.2) | collective-permute-done | bytes 786464 | tf_op jit(solution)/shard_map/ppermute | solution.py:21
  69.8 21.0 %collective-permute-done.4.refs_6_ = bf16[256,1536]{1,0:T(8,128)(2,1)} collective-permute-done((bf16[256,1536]{1,0:T(8,128)(2,1)S(1)}, bf16[256,1536]{1,0:T(8,128)(2,1)}, u32[]{:S(2)}, u32[]{:S(2)}) %collective-permute-start.4) | collective-permute-done | bytes 786464 | tf_op jit(solution)/shard_map/ppermute | solution.py:21
  90.8 9.7 %collective-permute-done.5.refs_7_ = bf16[256,1536]{1,0:T(8,128)(2,1)} collective-permute-done((bf16[256,1536]{1,0:T(8,128)(2,1)S(1)}, bf16[256,1536]{1,0:T(8,128)(2,1)}, u32[]{:S(2)}, u32[]{:S(2)}) %collective-permute-start.5) | collective-permute-done | bytes 786464 | tf_op jit(solution)/shard_map/ppermute | solution.py:21
  100.6 43.3 %shard_map.152 = (bf16[3072,256]{1,0:T(8,128)(2,1)}, bf16[256,3072]{1,0:T(8,128)(2,1)}, bf16[4,256,1536]{2,1,0:T(8,128)(2,1)}, bf16[4,256,1536]{2,1,0:T(8,128)(2...) custom-call(s32[97]{0:T(128)} %pad_add_fusion.index, bf16[256,1536]{1,0:T(8,128)(2,1)} %refs_0_.3, ...), custom_call_target="tpu_custom_call" | custom-call | flops 25769803776 | bytes 50331648 | tf_op jit(solution)/shard_map/pallas_call | solution.py:215
  146.3 3.2 pad_maximum_fusion.refs_4_
  153.9 4.6 %shard_map.153 = (bf16[2,12,256,256]{3,2,1,0:T(8,128)(2,1)}, bf16[1536,256]{1,0:T(8,128)(2,1)}) custom-call(bf16[256,1536]{1,0:T(8,128)(2,1)} %refs_0_.3, bf16[256,1536]{1,0:T(8,128)(2,1)} %copy-done.14, bf16[256,1536]{1,0:T(8,128)(2,1)} %collective-permute-done.1.refs_2_, bf16[256,1536]{1,0:T(8,128)(2,1)} %collective-permute-done.2.refs_3_), custom_call_target="tpu_custom_call" | custom-call | bytes 6291456 | tf_op jit(solution)/shard_map/pallas_call | solution.py:192
  159.7 3.6 collective-permute-start.11
  163.3 1.6 collective-permute-start.38
  165.0 57.2 %collective-permute-done.38 = bf16[384,256]{1,0:T(8,128)(2,1)S(1)} collective-permute-done((bf16[384,256]{1,0:T(8,128)(2,1)S(1)}, bf16[384,256]{1,0:T(8,128)(2,1)S(1)}, u32[]{:S(2)}, u32[]{:S(2)}) %collective-permute-start.38) | collective-permute-done | bytes 196640 | tf_op jit(solution)/shard_map/ppermute | solution.py:21
  224.4 5.0 %collective-permute-done.40 = bf16[384,256]{1,0:T(8,128)(2,1)S(1)} collective-permute-done((bf16[384,256]{1,0:T(8,128)(2,1)S(1)}, bf16[384,256]{1,0:T(8,128)(2,1)S(1)}, u32[]{:S(2)}, u32[]{:S(2)}) %collective-permute-start.40) | collective-permute-done | bytes 196640 | tf_op jit(solution)/shard_map/ppermute | solution.py:21
  230.1 4.1 collective-permute-start.16
  234.2 21.2 %collective-permute-done.14 = bf16[2,256,256]{2,1,0:T(8,128)(2,1)S(1)} collective-permute-done((bf16[2,256,256]{2,1,0:T(8,128)(2,1)S(1)}, bf16[2,256,256]{2,1,0:T(8,128)(2,1)S(1)}, u32[]{:S(2)}, u32[]{:S(2)}) %collective-permute-start.14) | collective-permute-done | bytes 262176 | tf_op jit(solution)/shard_map/ppermute | solution.py:21
  256.4 5.7 %dynamic-slice_bitcast_fusion = (bf16[12,256,256]{2,1,0:T(8,128)(2,1)}, bf16[12,256,256]{2,1,0:T(8,128)(2,1)}, bf16[12,256,256]{2,1,0:T(8,128)(2,1)}, bf16[12,256,256]{2,1,0:T(8,128)(2,1)}) fusion(bf16[2,12,256,256]{3,2,1,0:T(8,128)(2,1)} %get-tuple-element.24, s32[]{:T(128)S(6)} %select_n.79, s32[]{:T(128)S(6)} %select_n.77, s32[]{:T(128)S(6)} %select_n.75, ...), kind=kLoop, calls=%fused_computation.15 | loop fusion | bytes 12582928 | tf_op jit(solution)/shard_map/jit(dynamic_index_in_dim)/squeeze | solution.py:201
  262.3 10.1 %collective-permute-done.17 = bf16[256,1536]{1,0:T(8,128)(2,1)} collective-permute-done((bf16[256,1536]{1,0:T(8,128)(2,1)}, bf16[256,1536]{1,0:T(8,128)(2,1)}, u32[]{:S(2)}, u32[]{:S(2)}) %collective-permute-start.17) | collective-permute-done | bytes 786464 | tf_op jit(solution)/shard_map/ppermute | solution.py:21
  275.6 69.8 %collective-permute-done.39 = bf16[256,256]{1,0:T(8,128)(2,1)S(1)} collective-permute-done((bf16[256,256]{1,0:T(8,128)(2,1)S(1)}, bf16[256,256]{1,0:T(8,128)(2,1)S(1)}, u32[]{:S(2)}, u32[]{:S(2)}) %collective-permute-start.39) | collective-permute-done | bytes 131104 | tf_op jit(solution)/shard_map/ppermute | solution.py:21
  349.4 2.3 constant_dynamic-slice_fusion.3
  351.8 2.9 fusion.9
  355.8 3.4 fusion.5
  361.6 29.6 %collective-permute-done.20.refs_3_ = bf16[12,256,256]{2,1,0:T(8,128)(2,1)S(1)} collective-permute-done((bf16[12,256,256]{2,1,0:T(8,128)(2,1)S(1)}, bf16[12,256,256]{2,1,0:T(8,128)(2,1)S(1)}, u32[]{:S(2)}, u32[]{:S(2)}) %collective-permute-start.20) | collective-permute-done | bytes 1572896 | tf_op jit(solution)/shard_map/ppermute | solution.py:21
  393.4 16.8 %shard_map.154 = (bf16[4,256,3072]{2,1,0:T(8,128)(2,1)}, bf16[64,3072]{1,0:T(8,128)(2,1)}) custom-call(s32[97]{0:T(128)} %pad_add_fusion.index, bf16[12,256,256]{2,1,0:T(8,128)(2,1)} %get-tuple-element.35.refs_0_, bf16[12,256,256]{2,1,0:T(8,128)(2,1)} %collective-permute-done.18.refs_1_, bf16[12,256,256]{2,1,0:T(8,128)(2,1)} %collective-permute-done.19.refs_2_, ...), custom_call_target="tpu_custom_call" | custom-call | flops 6442450944 | bytes 18874368 | tf_op jit(solution)/shard_map/pallas_call | solution.py:278
  413.3 9.0 %collective-permute-done.44 = bf16[64,256]{0,1:T(8,128)(2,1)S(1)} collective-permute-done((bf16[64,256]{0,1:T(8,128)(2,1)S(1)}, bf16[64,256]{0,1:T(8,128)(2,1)S(1)}, u32[]{:S(2)}, u32[]{:S(2)}) %collective-permute-start.44) | collective-permute-done | bytes 32800 | tf_op jit(solution)/shard_map/ppermute | solution.py:21
  425.9 9.2 %collective-permute-done.43 = bf16[64,256]{0,1:T(8,128)(2,1)S(1)} collective-permute-done((bf16[64,256]{0,1:T(8,128)(2,1)S(1)}, bf16[64,256]{0,1:T(8,128)(2,1)S(1)}, u32[]{:S(2)}, u32[]{:S(2)}) %collective-permute-start.43) | collective-permute-done | bytes 32800 | tf_op jit(solution)/shard_map/ppermute | solution.py:21
  435.2 2.1 fusion.1
  438.4 14.6 %shard_map.155 = (bf16[4,768,1024]{2,1,0:T(8,128)(2,1)}, bf16[768,256]{1,0:T(8,128)(2,1)}) custom-call(s32[97]{0:T(128)} %pad_add_fusion.index, bf16[768,256]{1,0:T(8,128)(2,1)} %get-tuple-element.45.refs_0_, bf16[768,256]{1,0:T(8,128)(2,1)} %copy-done.29, bf16[768,256]{1,0:T(8,128)(2,1)} %copy-done.30, bf16[768,256]{1,0:T(8,128)(2,1)} %copy-done.31, ...), custom_call_target="tpu_custom_call" | custom-call | flops 6442450944 | bytes 18874368 | tf_op jit(solution)/shard_map/pallas_call | solution.py:261
  (175 shorter events, 44.2 us)
Async XLA Ops:
  6.8 28.3 %collective-permute-start = (bf16[256,1536]{1,0:T(8,128)(2,1)S(1)}, bf16[256,1536]{1,0:T(8,128)(2,1)S(1)}, u32[]{:S(2)}, u32[]{:S(2)}) collective-permute-start(bf16[256,1536]{1,0:T(8,128)(2,1)S(1)} %copy-done.6), channel_id=1, source_target_pairs={{0,4},{4,0},{8,12},{12,8},{16,20},{20,16},{24,28},{28,24},{1,5},{5... | collective-permute-start | bytes 2359304 | tf_op jit(solution)/shard_map/ppermute | solution.py:21
  24.1 37.5 %collective-permute-start.1 = (bf16[256,1536]{1,0:T(8,128)(2,1)S(1)}, bf16[256,1536]{1,0:T(8,128)(2,1)}, u32[]{:S(2)}, u32[]{:S(2)}) collective-permute-start(bf16[256,1536]{1,0:T(8,128)(2,1)S(1)} %copy-done.6), channel_id=1, source_target_pairs={{0,8},{4,12},{8,0},{12,4},{16,24},{20,28},{24,16},{28,20},{1,9},{5... | collective-permute-start | bytes 2359304 | tf_op jit(solution)/shard_map/ppermute | solution.py:21
  25.4 42.9 %collective-permute-start.2 = (bf16[256,1536]{1,0:T(8,128)(2,1)S(1)}, bf16[256,1536]{1,0:T(8,128)(2,1)}, u32[]{:S(2)}, u32[]{:S(2)}) collective-permute-start(bf16[256,1536]{1,0:T(8,128)(2,1)S(1)} %copy-done.6), channel_id=1, source_target_pairs={{0,16},{4,20},{8,24},{12,28},{16,0},{20,4},{24,8},{28,12},{1,17},{... | collective-permute-start | bytes 2359304 | tf_op jit(solution)/shard_map/ppermute | solution.py:21
  25.7 44.2 %collective-permute-start.3 = (bf16[256,1536]{1,0:T(8,128)(2,1)S(1)}, bf16[256,1536]{1,0:T(8,128)(2,1)}, u32[]{:S(2)}, u32[]{:S(2)}) collective-permute-start(bf16[256,1536]{1,0:T(8,128)(2,1)S(1)} %copy-done.1), channel_id=1, source_target_pairs={{0,4},{4,0},{8,12},{12,8},{16,20},{20,16},{24,28},{28,24},{1,5},{5... | collective-permute-start | bytes 2359304 | tf_op jit(solution)/shard_map/ppermute | solution.py:21
  34.5 56.4 %collective-permute-start.4 = (bf16[256,1536]{1,0:T(8,128)(2,1)S(1)}, bf16[256,1536]{1,0:T(8,128)(2,1)}, u32[]{:S(2)}, u32[]{:S(2)}) collective-permute-start(bf16[256,1536]{1,0:T(8,128)(2,1)S(1)} %copy-done.1), channel_id=1, source_target_pairs={{0,8},{4,12},{8,0},{12,4},{16,24},{20,28},{24,16},{28,20},{1,9},{5... | collective-permute-start | bytes 2359304 | tf_op jit(solution)/shard_map/ppermute | solution.py:21
  35.0 65.5 %collective-permute-start.5 = (bf16[256,1536]{1,0:T(8,128)(2,1)S(1)}, bf16[256,1536]{1,0:T(8,128)(2,1)}, u32[]{:S(2)}, u32[]{:S(2)}) collective-permute-start(bf16[256,1536]{1,0:T(8,128)(2,1)S(1)} %copy-done.1), channel_id=1, source_target_pairs={{0,16},{4,20},{8,24},{12,28},{16,0},{20,4},{24,8},{28,12},{1,17},{... | collective-permute-start | bytes 2359304 | tf_op jit(solution)/shard_map/ppermute | solution.py:21
  61.6 98.1 %collective-permute-start.24 = (bf16[64,256]{1,0:T(8,128)(2,1)S(1)}, bf16[64,256]{1,0:T(8,128)(2,1)S(1)}, u32[]{:S(2)}, u32[]{:S(2)}) collective-permute-start(bf16[64,256]{1,0:T(8,128)(2,1)S(1)} %bitcast.114), channel_id=1, source_target_pairs={{0,1},{1,0},{2,3},{3,2},{4,5},{5,4},{6,7},{7,6},{8,9},{9,8},{10,11... | collective-permute-start | bytes 98312 | tf_op jit(solution)/shard_map/ppermute | solution.py:21
  68.3 95.0 %collective-permute-start.25 = (bf16[64,256]{1,0:T(8,128)(2,1)S(1)}, bf16[64,256]{1,0:T(8,128)(2,1)S(1)}, u32[]{:S(2)}, u32[]{:S(2)}) collective-permute-start(bf16[64,256]{1,0:T(8,128)(2,1)S(1)} %bitcast.113), channel_id=1, source_target_pairs={{0,2},{1,3},{2,0},{3,1},{4,6},{5,7},{6,4},{7,5},{8,10},{9,11},{10,... | collective-permute-start | bytes 98312 | tf_op jit(solution)/shard_map/ppermute | solution.py:21
  69.8 93.5 %collective-permute-start.26 = (bf16[64,256]{1,0:T(8,128)(2,1)S(1)}, bf16[64,256]{1,0:T(8,128)(2,1)S(1)}, u32[]{:S(2)}, u32[]{:S(2)}) collective-permute-start(bf16[64,256]{1,0:T(8,128)(2,1)S(1)} %bitcast.112), channel_id=1, source_target_pairs={{0,3},{1,2},{2,1},{3,0},{4,7},{5,6},{6,5},{7,4},{8,11},{9,10},{10,... | collective-permute-start | bytes 98312 | tf_op jit(solution)/shard_map/ppermute | solution.py:21
  149.5 198.8 %collective-permute-start.31 = (bf16[4,256,1536]{2,1,0:T(8,128)(2,1)}, bf16[4,256,1536]{2,1,0:T(8,128)(2,1)}, u32[]{:S(2)}, u32[]{:S(2)}) collective-permute-start(bf16[4,256,1536]{2,1,0:T(8,128)(2,1)} %pad_maximum_fusion.refs_4_), channel_id=1, source_target_pairs={{0,2},{1,3},{2,0},{3,1},{4,6},{5,7},{6,4},{7,5},{8,10},{9,11},{10,... | collective-permute-start | bytes 9437192 | tf_op jit(solution)/shard_map/ppermute | solution.py:21
  159.7 70.4 %collective-permute-start.11 = (bf16[256,1536]{1,0:T(8,128)(2,1)}, bf16[256,1536]{1,0:T(8,128)(2,1)S(1)}, u32[]{:S(2)}, u32[]{:S(2)}) collective-permute-start(bf16[256,1536]{1,0:T(8,128)(2,1)} %get-tuple-element.40), channel_id=1, source_target_pairs={{0,16},{4,20},{8,24},{12,28},{16,0},{20,4},{24,8},{28,12},{1,17},{... | collective-permute-start | bytes 2359304 | tf_op jit(solution)/shard_map/ppermute | solution.py:21
  163.3 66.8 %collective-permute-start.10 = (bf16[256,1536]{1,0:T(8,128)(2,1)}, bf16[256,1536]{1,0:T(8,128)(2,1)S(1)}, u32[]{:S(2)}, u32[]{:S(2)}) collective-permute-start(bf16[256,1536]{1,0:T(8,128)(2,1)} %get-tuple-element.41), channel_id=1, source_target_pairs={{0,8},{4,12},{8,0},{12,4},{16,24},{20,28},{24,16},{28,20},{1,9},{5... | collective-permute-start | bytes 2359304 | tf_op jit(solution)/shard_map/ppermute | solution.py:21
  163.3 58.9 %collective-permute-start.38 = (bf16[384,256]{1,0:T(8,128)(2,1)S(1)}, bf16[384,256]{1,0:T(8,128)(2,1)S(1)}, u32[]{:S(2)}, u32[]{:S(2)}) collective-permute-start(bf16[384,256]{1,0:T(8,128)(2,1)S(1)} %get-tuple-element.47), channel_id=1, source_target_pairs={{0,2},{1,3},{2,0},{3,1},{4,6},{5,7},{6,4},{7,5},{8,10},{9,11},{10,... | collective-permute-start | bytes 589832 | tf_op jit(solution)/shard_map/ppermute | solution.py:21
  164.9 57.4 %collective-permute-start.36 = (bf16[384,256]{1,0:T(8,128)(2,1)S(1)}, bf16[384,256]{1,0:T(8,128)(2,1)S(1)}, u32[]{:S(2)}, u32[]{:S(2)}) collective-permute-start(bf16[384,256]{1,0:T(8,128)(2,1)S(1)} %get-tuple-element.48), channel_id=1, source_target_pairs={{0,1},{1,0},{2,3},{3,2},{4,5},{5,4},{6,7},{7,6},{8,9},{9,8},{10,11... | collective-permute-start | bytes 589832 | tf_op jit(solution)/shard_map/ppermute | solution.py:21
  222.9 32.5 %collective-permute-start.14 = (bf16[2,256,256]{2,1,0:T(8,128)(2,1)S(1)}, bf16[2,256,256]{2,1,0:T(8,128)(2,1)S(1)}, u32[]{:S(2)}, u32[]{:S(2)}) collective-permute-start(bf16[2,256,256]{2,1,0:T(8,128)(2,1)S(1)} %add_convert_fusion.1), channel_id=1, source_target_pairs={{0,16},{4,20},{8,24},{12,28},{16,0},{20,4},{24,8},{28,12},{1,17},{... | collective-permute-start | bytes 786440 | tf_op jit(solution)/shard_map/ppermute | solution.py:21
  229.4 32.8 %collective-permute-start.9 = (bf16[256,1536]{1,0:T(8,128)(2,1)}, bf16[256,1536]{1,0:T(8,128)(2,1)}, u32[]{:S(2)}, u32[]{:S(2)}) collective-permute-start(bf16[256,1536]{1,0:T(8,128)(2,1)} %get-tuple-element.39), channel_id=1, source_target_pairs={{0,4},{4,0},{8,12},{12,8},{16,20},{20,16},{24,28},{28,24},{1,5},{5... | collective-permute-start | bytes 2359304 | tf_op jit(solution)/shard_map/ppermute | solution.py:21
  230.1 42.3 %collective-permute-start.17 = (bf16[256,1536]{1,0:T(8,128)(2,1)}, bf16[256,1536]{1,0:T(8,128)(2,1)}, u32[]{:S(2)}, u32[]{:S(2)}) collective-permute-start(bf16[256,1536]{1,0:T(8,128)(2,1)} %get-tuple-element.37), channel_id=1, source_target_pairs={{0,16},{4,20},{8,24},{12,28},{16,0},{20,4},{24,8},{28,12},{1,17},{... | collective-permute-start | bytes 2359304 | tf_op jit(solution)/shard_map/ppermute | solution.py:21
  230.1 42.9 %collective-permute-start.16 = (bf16[256,1536]{1,0:T(8,128)(2,1)}, bf16[256,1536]{1,0:T(8,128)(2,1)}, u32[]{:S(2)}, u32[]{:S(2)}) collective-permute-start(bf16[256,1536]{1,0:T(8,128)(2,1)} %get-tuple-element.38), channel_id=1, source_target_pairs={{0,8},{4,12},{8,0},{12,4},{16,24},{20,28},{24,16},{28,20},{1,9},{5... | collective-permute-start | bytes 2359304 | tf_op jit(solution)/shard_map/ppermute | solution.py:21
  255.4 20.2 %collective-permute-start.15 = (bf16[256,1536]{1,0:T(8,128)(2,1)}, bf16[256,1536]{1,0:T(8,128)(2,1)}, u32[]{:S(2)}, u32[]{:S(2)}) collective-permute-start(bf16[256,1536]{1,0:T(8,128)(2,1)} %get-tuple-element.36), channel_id=1, source_target_pairs={{0,4},{4,0},{8,12},{12,8},{16,20},{20,16},{24,28},{28,24},{1,5},{5... | collective-permute-start | bytes 2359304 | tf_op jit(solution)/shard_map/ppermute | solution.py:21
  262.2 92.6 %collective-permute-start.18 = (bf16[12,256,256]{2,1,0:T(8,128)(2,1)}, bf16[12,256,256]{2,1,0:T(8,128)(2,1)}, u32[]{:S(2)}, u32[]{:S(2)}) collective-permute-start(bf16[12,256,256]{2,1,0:T(8,128)(2,1)} %get-tuple-element.34), channel_id=1, source_target_pairs={{0,1},{1,0},{2,3},{3,2},{4,5},{5,4},{6,7},{7,6},{8,9},{9,8},{10,11... | collective-permute-start | bytes 4718600 | tf_op jit(solution)/shard_map/ppermute | solution.py:21
  272.3 82.6 %collective-permute-start.19 = (bf16[12,256,256]{2,1,0:T(8,128)(2,1)}, bf16[12,256,256]{2,1,0:T(8,128)(2,1)}, u32[]{:S(2)}, u32[]{:S(2)}) collective-permute-start(bf16[12,256,256]{2,1,0:T(8,128)(2,1)} %get-tuple-element.33), channel_id=1, source_target_pairs={{0,2},{1,3},{2,0},{3,1},{4,6},{5,7},{6,4},{7,5},{8,10},{9,11},{10,... | collective-permute-start | bytes 4718600 | tf_op jit(solution)/shard_map/ppermute | solution.py:21
  273.0 82.1 %collective-permute-start.22 = (bf16[256,3072]{1,0:T(8,128)(2,1)}, bf16[256,3072]{1,0:T(8,128)(2,1)}, u32[]{:S(2)}, u32[]{:S(2)}) collective-permute-start(bf16[256,3072]{1,0:T(8,128)(2,1)} %get-tuple-element.25.refs_4_), channel_id=1, source_target_pairs={{0,2},{1,3},{2,0},{3,1},{4,6},{5,7},{6,4},{7,5},{8,10},{9,11},{10,... | collective-permute-start | bytes 4718600 | tf_op jit(solution)/shard_map/ppermute | solution.py:21
  275.6 69.8 %collective-permute-start.39 = (bf16[256,256]{1,0:T(8,128)(2,1)S(1)}, bf16[256,256]{1,0:T(8,128)(2,1)S(1)}, u32[]{:S(2)}, u32[]{:S(2)}) collective-permute-start(bf16[256,256]{1,0:T(8,128)(2,1)S(1)} %get-tuple-element.50), channel_id=1, source_target_pairs={{0,2},{1,3},{2,0},{3,1},{4,6},{5,7},{6,4},{7,5},{8,10},{9,11},{10,... | collective-permute-start | bytes 393224 | tf_op jit(solution)/shard_map/ppermute | solution.py:21
  348.1 63.6 %collective-permute-start.30 = (bf16[4,256,1536]{2,1,0:T(8,128)(2,1)}, bf16[4,256,1536]{2,1,0:T(8,128)(2,1)}, u32[]{:S(2)}, u32[]{:S(2)}) collective-permute-start(bf16[4,256,1536]{2,1,0:T(8,128)(2,1)} %pad_maximum_fusion.refs_4_), channel_id=1, source_target_pairs={{0,1},{1,0},{2,3},{3,2},{4,5},{5,4},{6,7},{7,6},{8,9},{9,8},{10,11... | collective-permute-start | bytes 9437192 | tf_op jit(solution)/shard_map/ppermute | solution.py:21
  348.3 75.4 %collective-permute-start.32 = (bf16[4,256,1536]{2,1,0:T(8,128)(2,1)}, bf16[4,256,1536]{2,1,0:T(8,128)(2,1)}, u32[]{:S(2)}, u32[]{:S(2)}) collective-permute-start(bf16[4,256,1536]{2,1,0:T(8,128)(2,1)} %collective-permute-done.31.refs_6_), channel_id=1, source_target_pairs={{0,1},{1,0},{2,3},{3,2},{4,5},{5,4},{6,7},{7,6},{8,9},{9,8},{10,11... | collective-permute-start | bytes 9437192 | tf_op jit(solution)/shard_map/ppermute | solution.py:21
  354.8 36.7 %collective-permute-start.21 = (bf16[256,3072]{1,0:T(8,128)(2,1)}, bf16[256,3072]{1,0:T(8,128)(2,1)S(1)}, u32[]{:S(2)}, u32[]{:S(2)}) collective-permute-start(bf16[256,3072]{1,0:T(8,128)(2,1)} %get-tuple-element.25.refs_4_), channel_id=1, source_target_pairs={{0,1},{1,0},{2,3},{3,2},{4,5},{5,4},{6,7},{7,6},{8,9},{9,8},{10,11... | collective-permute-start | bytes 4718600 | tf_op jit(solution)/shard_map/ppermute | solution.py:21
  354.9 36.2 %collective-permute-start.20 = (bf16[12,256,256]{2,1,0:T(8,128)(2,1)S(1)}, bf16[12,256,256]{2,1,0:T(8,128)(2,1)S(1)}, u32[]{:S(2)}, u32[]{:S(2)}) collective-permute-start(bf16[12,256,256]{2,1,0:T(8,128)(2,1)S(1)} %copy-done.7), channel_id=1, source_target_pairs={{0,3},{1,2},{2,1},{3,0},{4,7},{5,6},{6,5},{7,4},{8,11},{9,10},{10,... | collective-permute-start | bytes 4718600 | tf_op jit(solution)/shard_map/ppermute | solution.py:21
  355.2 36.4 %collective-permute-start.23 = (bf16[256,3072]{1,0:T(8,128)(2,1)}, bf16[256,3072]{1,0:T(8,128)(2,1)S(1)}, u32[]{:S(2)}, u32[]{:S(2)}) collective-permute-start(bf16[256,3072]{1,0:T(8,128)(2,1)} %collective-permute-done.22.refs_6_), channel_id=1, source_target_pairs={{0,1},{1,0},{2,3},{3,2},{4,5},{5,4},{6,7},{7,6},{8,9},{9,8},{10,11... | collective-permute-start | bytes 4718600 | tf_op jit(solution)/shard_map/ppermute | solution.py:21
  391.2 34.7 %collective-permute-start.34 = (bf16[256,256]{1,0:T(8,128)(2,1)S(1)}, bf16[256,256]{1,0:T(8,128)(2,1)S(1)}, u32[]{:S(2)}, u32[]{:S(2)}) collective-permute-start(bf16[256,256]{1,0:T(8,128)(2,1)S(1)} %copy-done.20), channel_id=1, source_target_pairs={{0,2},{1,3},{2,0},{3,1},{4,6},{5,7},{6,4},{7,5},{8,10},{9,11},{10,... | collective-permute-start | bytes 393224 | tf_op jit(solution)/shard_map/ppermute | solution.py:21
  391.5 45.8 %collective-permute-start.27 = (bf16[768,256]{1,0:T(8,128)(2,1)S(1)}, bf16[768,256]{1,0:T(8,128)(2,1)S(1)}, u32[]{:S(2)}, u32[]{:S(2)}) collective-permute-start(bf16[768,256]{1,0:T(8,128)(2,1)S(1)} %get-tuple-element.44), channel_id=1, source_target_pairs={{0,1},{1,0},{2,3},{3,2},{4,5},{5,4},{6,7},{7,6},{8,9},{9,8},{10,11... | collective-permute-start | bytes 1179656 | tf_op jit(solution)/shard_map/ppermute | solution.py:21
  391.6 18.6 %collective-permute-start.42 = (bf16[64,256]{0,1:T(8,128)(2,1)S(1)}, bf16[64,256]{0,1:T(8,128)(2,1)S(1)}, u32[]{:S(2)}, u32[]{:S(2)}) collective-permute-start(bf16[64,256]{0,1:T(8,128)(2,1)S(1)} %get-tuple-element.55), channel_id=1, source_target_pairs={{0,1},{1,0},{2,3},{3,2},{4,5},{5,4},{6,7},{7,6},{8,9},{9,8},{10,11... | collective-permute-start | bytes 98312 | tf_op jit(solution)/shard_map/ppermute | solution.py:21
  410.2 27.1 %collective-permute-start.28 = (bf16[768,256]{1,0:T(8,128)(2,1)S(1)}, bf16[768,256]{1,0:T(8,128)(2,1)S(1)}, u32[]{:S(2)}, u32[]{:S(2)}) collective-permute-start(bf16[768,256]{1,0:T(8,128)(2,1)S(1)} %get-tuple-element.43), channel_id=1, source_target_pairs={{0,2},{1,3},{2,0},{3,1},{4,6},{5,7},{6,4},{7,5},{8,10},{9,11},{10,... | collective-permute-start | bytes 1179656 | tf_op jit(solution)/shard_map/ppermute | solution.py:21
  (51 other events, 634.3 us)
